TPU v7x, 1024 devices: a whole 8x8x8 slice. The times are simulated.
1024 devices in a mesh: dp: 128 (over z, y_lo, x), peer: 8 (over y_hi, core).
Axes of the slice: x: 8, y: 8 (y_hi: 4, y_lo: 2; y = y_hi * 2 + y_lo), z: 8, core: 2. Of those that a mesh axis runs over, the one named last changes fastest.
Arguments:
- grads: bfloat16 [128, 2, 128, 8192], P('dp', None, 'peer'), may hold values from -0.796875 to 0.796875
- params: float32 [2, 8, 131072], P(None, 'peer', 'dp'), may hold values from -6 to 6
- moment1: float32 [2, 8, 131072], P(None, 'peer', 'dp'), may hold values from -2 to 2
- moment2: float32 [2, 8, 131072], P(None, 'peer', 'dp'), may hold values from 0.01 to 1
- base_params: float32 [2, 8, 131072], P(None, 'peer', 'dp'), may hold values from -6 to 6
- base_m1: float32 [2, 8, 131072], P(None, 'peer', 'dp'), may hold values from -2 to 2
- base_m2: float32 [2, 8, 131072], P(None, 'peer', 'dp'), may hold values from 0.01 to 1
- coef_num: int32 [4, 8], replicated, may hold values from -8 to 8, as said below
Outputs:
- new_params: float32 [2, 8, 131072], P(None, 'peer', 'dp')
- new_m1: float32 [2, 8, 131072], P(None, 'peer', 'dp')
- new_m2: float32 [2, 8, 131072], P(None, 'peer', 'dp')
- weights: bfloat16 [2, 128, 8192], P(None, 'peer')
- parity: float32 [4, 3, 2, 131072], P(None, None, None, ('dp', 'peer'))
Inputs may be any that keep to these rules, and one draw needn't show every extreme that they name: `coef_num`: never zero.
All inputs are finite; a program needn't handle non-finite values.
Results may differ from a plain program's by a relative error of at most 0.001.
Values may be sent and summed in bfloat16 or wider, within the bound.
No kernel may reach another device: no remote copies, remote signals or barrier semaphores. Data moves between devices by JAX's collectives and lax.ppermute only.
A program may use at most 32 MiB of HBM per device.

v0:
```python
import jax
import jax.numpy as jnp
from jax import lax
from jax.sharding import PartitionSpec as P


def adamw(g, params, moment1, moment2):
    new_m1 = 0.9 * moment1 + 0.1 * g
    new_m2 = 0.95 * moment2 + 0.05 * g * g
    fix_one = 1.0 - 0.9**10
    fix_two = 1.0 - 0.95**10
    new_params = params - 0.01 * (
        new_m1 / fix_one / (jnp.sqrt(new_m2 / fix_two) + 1e-08) + 0.1 * params
    )
    return (new_params, new_m1, new_m2)


def body(grads, params, moment1, moment2, base_params, base_m1, base_m2, coef_num):
    layers = grads.shape[1]
    rows = grads.shape[2]
    width = grads.shape[3]
    groups = lax.axis_size("dp")
    span = params.shape[2]
    partial_sums = grads.reshape(layers, groups, span).astype(jnp.float32)
    g = lax.psum_scatter(partial_sums, "dp", scatter_dimension=1, tiled=True)
    new_params, new_m1, new_m2 = adamw(g, params, moment1, moment2)
    gathered = lax.all_gather(new_params.astype(jnp.bfloat16), "dp", axis=2, tiled=True)
    weights = gathered.reshape(layers, rows, width)
    delta = jnp.stack([new_params - base_params, new_m1 - base_m1, new_m2 - base_m2], 0).reshape(
        3, layers, span
    )
    coef = coef_num.astype(jnp.float32) / 8.0
    member = lax.axis_index("peer")
    picker = (jnp.arange(coef.shape[1], dtype=jnp.int32) == member).astype(jnp.float32)
    column = jnp.sum(coef * picker[None, :], axis=1)
    terms = column[:, None, None, None] * delta[None]
    parity = lax.psum_scatter(terms, "peer", scatter_dimension=3, tiled=True)
    return (new_params, new_m1, new_m2, weights, parity)


def solution(mesh):
    placed = (
        P("dp", None, "peer", None),
        P(None, "peer", "dp"),
        P(None, "peer", "dp"),
        P(None, "peer", "dp"),
        P(None, "peer", "dp"),
        P(None, "peer", "dp"),
        P(None, "peer", "dp"),
        P(),
    )
    return jax.shard_map(
        body,
        mesh=mesh,
        in_specs=placed,
        out_specs=(
            P(None, "peer", "dp"),
            P(None, "peer", "dp"),
            P(None, "peer", "dp"),
            P(None, "peer", None),
            P(None, None, None, ("dp", "peer")),
        ),
        check_vma=False,
    )
```

profile of v0, /device:TPU:32, one launch (start us, length us, event | category | flops | bytes accessed | tf_op | source)
XLA Modules:
  0.0 1558.8 jit_solution(15721406680087494482)
XLA Ops:
  7.2 0.0 all-reduce.3.cloned.1.call-start
  7.2 1.3 reshape.24
  8.5 1.8 copy.24
  10.3 0.0 all-reduce.3.cloned.1.call-update
  10.3 0.0 reduce-scatter.4.cloned.1.call-start
  10.4 1.3 dynamic-slice
  11.7 0.8 multiply_reduce_fusion
  12.5 1210.7 %all-reduce.3.cloned.1.call-done = f32[2,128,1024]{2,0,1:T(2,128)} async-done(((f32[2,128,1024]{2,0,1:T(2,128)}), f32[2,128,1024]{2,0,1:T(2,128)}) %all-reduce.3.cloned.1.call-update) | async-done | bytes 1048592
  1223.2 1.5 fusion.3
  1224.7 0.6 copy.31
  1225.3 0.6 copy.32
  1225.9 0.6 copy.33
  1226.5 0.7 fusion.1
  1227.2 0.1 broadcast_multiply_fusion
  1227.3 6.2 copy.34
  1233.5 10.1 reshape.25
  1243.6 0.0 reduce-scatter.4.cloned.1.call-update
  1243.7 304.3 %all_gather.3 = bf16[2,1,131072]{2,0,1:T(2,128)(2,1)S(1)} all-gather(bf16[2,1,1024]{2,0,1:T(2,128)(2,1)S(1)} %convert_element_type.19), channel_id=1, replica_groups=mesh['dp'=128,'peer'=8] {'dp'}, dimensions={2}, use_global_device_ids=true | all-gather | bytes 528384 | tf_op jit(solution)/shard_map/all_gather | solution.py:27
  1548.0 1.1 copy.57
  1549.1 0.0 reduce-scatter.4.cloned.1.call-done
  1549.1 1.8 reshape.26
  1550.9 1.1 copy.35
  (3 shorter events, 0.0 us)
Async XLA Ops:
  7.2 1216.0 %all-reduce.3.cloned.1.call-start = ((), (), s32[]{:S(2)}) async-start(), calls=%async_computation.2 | async-start | bytes 2097152
  10.3 1538.7 %reduce-scatter.4.cloned.1.call-start = ((), (), s32[]{:S(2)}) async-start(), calls=%async_computation.1 | async-start | bytes 589824
Sparse Core Ops, SparseCore 0:
  11.5 1211.6 all-reduce.2
  1243.8 30.4 reduce-scatter.3
where the time goes:
time: 1560 us
  waiting for transfers between devices  1210 us (78%)
  blocking collectives  304 us (19%)
  local copies, waits for them, and re-layouts  26.5 us (2%)
    unnamed x4, waiting for transfers between devices  1210 us
    all_gather x1, blocking collectives, body(): lax.all_gather(new_params.astype(jnp.bfloat16), 'dp', axis=2, tiled=True)  304 us
  transfers between devices with their start and end apart: 2, of which 1 were waited for; matrix products, arithmetic and copies ran while one was open for 0% of the time, Pallas kernels for 0%

commit v1 on v0

v1 whole, which is shorter than its diff:
```python
import jax
import jax.numpy as jnp
from jax import lax
from jax.sharding import PartitionSpec as P

LANES = 128


def adamw(g, params, moment1, moment2):
    new_m1 = 0.9 * moment1 + 0.1 * g
    new_m2 = 0.95 * moment2 + 0.05 * g * g
    fix_one = 1.0 - 0.9**10
    fix_two = 1.0 - 0.95**10
    new_params = params - 0.01 * (
        new_m1 / fix_one / (jnp.sqrt(new_m2 / fix_two) + 1e-08) + 0.1 * params
    )
    return (new_params, new_m1, new_m2)


def body(grads, params, moment1, moment2, base_params, base_m1, base_m2, coef_num):
    _, layers, rows, width = grads.shape
    groups = lax.axis_size("dp")
    peers = lax.axis_size("peer")
    span = params.shape[2]
    per_row = width // span
    blocks = span // LANES
    tall = (layers * blocks, LANES)

    pieces = grads.reshape(layers, rows, per_row, blocks, LANES)
    pieces = pieces.transpose(1, 2, 0, 3, 4).reshape(groups, *tall)
    arrived = lax.all_to_all(pieces, "dp", 0, 0, tiled=True)
    g = jnp.sum(arrived.astype(jnp.float32), axis=0)

    new_params, new_m1, new_m2 = adamw(
        g, params.reshape(tall), moment1.reshape(tall), moment2.reshape(tall)
    )

    mine = new_params.astype(jnp.bfloat16)
    gathered = lax.all_to_all(
        jnp.broadcast_to(mine[None], (groups, *tall)), "dp", 0, 0, tiled=True
    )
    weights = gathered.reshape(rows, per_row, layers, blocks, LANES)
    weights = weights.transpose(2, 0, 1, 3, 4).reshape(layers, rows, width)

    delta = jnp.stack(
        [
            new_params - base_params.reshape(tall),
            new_m1 - base_m1.reshape(tall),
            new_m2 - base_m2.reshape(tall),
        ],
        0,
    ).reshape(3 * layers, blocks, LANES)
    delta = delta.reshape(3 * layers, peers, -1).transpose(1, 0, 2)
    deltas = lax.all_to_all(delta, "peer", 0, 0, tiled=True)
    coef = coef_num.astype(jnp.float32) / 8.0
    parity = jnp.sum(coef[:, :, None, None] * deltas[None], axis=1)
    parity = parity.reshape(coef.shape[0], 3, layers, span // peers)

    own = params.shape
    return (new_params.reshape(own), new_m1.reshape(own), new_m2.reshape(own), weights, parity)


def solution(mesh):
    state = P(None, "peer", "dp")
    return jax.shard_map(
        body,
        mesh=mesh,
        in_specs=(P("dp", None, "peer", None),) + (state,) * 6 + (P(),),
        out_specs=(
            state,
            state,
            state,
            P(None, "peer", None),
            P(None, None, None, ("dp", "peer")),
        ),
        check_vma=False,
    )
```

time: 1560 us -> 93.5 us (0.06)
  the two profiles are of different devices: /device:TPU:32 before, /device:TPU:2 now
where the time goes in v1:
time: 93.5 us; the launch traced here: 93 us
  blocking collectives  44.8 us (48%)
  waiting for transfers between devices  27.9 us (30%)
  starting transfers between devices  12.8 us (14%)
  local copies, waits for them, and re-layouts  5.8 us (6%)
  other arithmetic  0.95 us (1%)
    all_to_all x1, blocking collectives, body(): arrived = lax.all_to_all(pieces, 'dp', 0, 0, tiled=True)  44.8 us
    all_to_all x1, waiting for transfers between devices, body(): lax.all_to_all(jnp.broadcast_to(mine[None], (groups, *tall)), 'dp', 0, 0,...  20 us
    all_to_all x1, waiting for transfers between devices, body(): deltas = lax.all_to_all(delta, 'peer', 0, 0, tiled=True)  7.91 us
    all_to_all x1, starting transfers between devices, body(): deltas = lax.all_to_all(delta, 'peer', 0, 0, tiled=True)  6.66 us
    all_to_all x1, starting transfers between devices, body(): lax.all_to_all(jnp.broadcast_to(mine[None], (groups, *tall)), 'dp', 0, 0,...  6.13 us
    unnamed x16, local copies, waits for them, and re-layouts  3.05 us
  transfers between devices with their start and end apart: 2, of which 2 were waited for; matrix products, arithmetic and copies ran while one was open for 1% of the time, Pallas kernels for 0%

profile of v1, /device:TPU:2, one launch (start us, length us, event | category | flops | bytes accessed | tf_op | source)
XLA Modules:
  0.0 93.0 jit_solution(13044404103359943128)
XLA Ops:
  0.6 1.2 %copy.39 = bf16[4,8,64,128]{3,2,1,0:T(8,128)(2,1)S(1)} copy(bf16[4,8,64,128]{3,1,2,0:T(8,128)(2,1)} %bitcast.70) | data formatting | bytes 1048576
  1.8 0.1 copy.30
  1.9 44.8 %all_to_all.15 = bf16[128,16,128]{2,1,0:T(8,128)(2,1)S(1)} all-to-all(bf16[128,16,128]{2,1,0:T(8,128)(2,1)S(1)} %bitcast.68), channel_id=1, replica_groups=mesh['dp'=128,'peer'=8] {'dp'}, dimensions={0} | all-to-all | bytes 1048576 | tf_op jit(solution)/shard_map/all_to_all | solution.py:31
  46.7 0.0 copy-start
  46.7 0.0 copy-start.1
  46.7 0.0 copy-start.2
  46.7 0.1 convert_reduce_fusion
  46.9 0.6 copy-done
  47.4 0.0 copy-done.1
  47.4 0.0 copy-done.2
  47.4 0.0 copy-start.4
  47.4 0.0 copy-start.5
  47.4 0.7 multiply_subtract_fusion
  48.1 0.0 copy-start.3
  48.1 0.0 copy-done.4
  48.1 0.0 copy-done.5
  48.2 0.7 copy-done.3
  48.9 0.6 copy.35
  49.5 6.7 %all-to-all-start.2 = ((f32[8,6,128]{2,1,0:T(8,128)}), f32[8,6,128]{2,1,0:T(8,128)S(1)}, u32[]{:S(2)}, u32[]{:S(2)}) async-start(f32[8,6,128]{2,1,0:T(8,128)} %copy.35), calls=%async_computation.2 | async-start | bytes 65536 | tf_op jit(solution)/shard_map/all_to_all | solution.py:54
  56.2 7.9 %all-to-all-done.2 = f32[8,6,128]{2,1,0:T(8,128)S(1)} async-done(((f32[8,6,128]{2,1,0:T(8,128)}), f32[8,6,128]{2,1,0:T(8,128)S(1)}, u32[]{:S(2)}, u32[]{:S(2)}) %all-to-all-start.2) | async-done | bytes 24608 | tf_op jit(solution)/shard_map/all_to_all | solution.py:54
  64.1 0.9 broadcast_in_dim.2
  64.9 0.0 copy-start.6
  64.9 6.1 %all-to-all-start.1 = ((bf16[128,16,128]{2,1,0:T(8,128)(2,1)}), bf16[128,16,128]{2,1,0:T(8,128)(2,1)S(1)}, u32[]{:S(2)}, u32[]{:S(2)}) async-start(bf16[128,16,128]{2,1,0:T(8,128)(2,1)} %broadcast_in_dim.2), calls=%async_computation.1 | async-start | bytes 1048576 | tf_op jit(solution)/shard_map/all_to_all | solution.py:39
  71.1 0.0 copy-done.6
  71.1 0.1 multiply_reduce_fusion
  71.2 0.6 copy.38
  71.8 20.0 %all-to-all-done.1 = bf16[128,16,128]{2,1,0:T(8,128)(2,1)S(1)} async-done(((bf16[128,16,128]{2,1,0:T(8,128)(2,1)}), bf16[128,16,128]{2,1,0:T(8,128)(2,1)S(1)}, u32[]{:S(2)}, u32[]{:S(2)}) %all-to-all-start.1) | async-done | bytes 524320 | tf_op jit(solution)/shard_map/all_to_all | solution.py:39
  91.8 0.1 copy.34
  92.0 1.0 %reshape.230 = bf16[2,16,8192]{2,1,0:T(8,128)(2,1)} reshape(bf16[2,16,8,8,128]{4,3,2,1,0:T(8,128)(2,1)S(1)} %copy.34) | data formatting | bytes 1048576 | tf_op jit(solution)/shard_map/reshape | solution.py:43
  (6 shorter events, 0.1 us)
Async XLA Ops:
  46.7 0.7 copy-start
  46.7 0.7 copy-start.1
  46.7 0.7 copy-start.2
  47.4 0.7 copy-start.4
  47.4 0.7 copy-start.5
  48.1 0.7 copy-start.3
  49.5 14.6 %all-to-all-start.2 = ((f32[8,6,128]{2,1,0:T(8,128)}), f32[8,6,128]{2,1,0:T(8,128)S(1)}, u32[]{:S(2)}, u32[]{:S(2)}) async-start(f32[8,6,128]{2,1,0:T(8,128)} %copy.35), calls=%async_computation.2 | async-start | bytes 65536 | tf_op jit(solution)/shard_map/all_to_all | solution.py:54
  64.9 6.1 %copy-start.6 = (s32[4,8]{1,0:T(4,128)S(1)}, s32[4,8]{1,0:T(4,128)}, u32[]{:S(2)}) copy-start(s32[4,8]{1,0:T(4,128)} %param.15) | copy-start | bytes 388
  64.9 26.9 %all-to-all-start.1 = ((bf16[128,16,128]{2,1,0:T(8,128)(2,1)}), bf16[128,16,128]{2,1,0:T(8,128)(2,1)S(1)}, u32[]{:S(2)}, u32[]{:S(2)}) async-start(bf16[128,16,128]{2,1,0:T(8,128)(2,1)} %broadcast_in_dim.2), calls=%async_computation.1 | async-start | bytes 1048576 | tf_op jit(solution)/shard_map/all_to_all | solution.py:39

commit v2 on v1

v2 whole, which is shorter than its diff:
```python
import jax
import jax.numpy as jnp
from jax import lax
from jax.experimental import pallas as pl
from jax.experimental.pallas import tpu as pltpu
from jax.sharding import PartitionSpec as P

LANES = 128


def adamw(g, params, moment1, moment2):
    new_m1 = 0.9 * moment1 + 0.1 * g
    new_m2 = 0.95 * moment2 + 0.05 * g * g
    fix_one = 1.0 - 0.9**10
    fix_two = 1.0 - 0.95**10
    new_params = params - 0.01 * (
        new_m1 / fix_one / (jnp.sqrt(new_m2 / fix_two) + 1e-08) + 0.1 * params
    )
    return (new_params, new_m1, new_m2)


def update_kernel(
    arrived, params, moment1, moment2, base_params, base_m1, base_m2,
    new_params, new_m1, new_m2, spread, delta,
):
    layers = 2
    peers = delta.shape[0]
    g = jnp.sum(arrived[...].astype(jnp.float32), axis=0)
    p, m1, m2 = adamw(g, params[...], moment1[...], moment2[...])
    spread[...] = jnp.broadcast_to(p.astype(jnp.bfloat16)[None], spread.shape)
    new_params[...] = p
    new_m1[...] = m1
    new_m2[...] = m2
    changes = (p - base_params[...], m1 - base_m1[...], m2 - base_m2[...])
    for s, change in enumerate(changes):
        for l in range(layers):
            for j in range(peers):
                delta[j, s * layers + l, :] = change[l * peers + j, :]


def update(arrived, *state):
    groups = arrived.shape[0]
    tall = arrived.shape[1:]
    whole = pl.BlockSpec(memory_space=pltpu.VMEM)
    f32 = jax.ShapeDtypeStruct(tall, jnp.float32)
    return pl.pallas_call(
        update_kernel,
        out_shape=(
            f32,
            f32,
            f32,
            jax.ShapeDtypeStruct((groups, *tall), jnp.bfloat16),
            jax.ShapeDtypeStruct((8, 6, LANES), jnp.float32),
        ),
        in_specs=[whole] * 7,
        out_specs=(whole,) * 5,
        compiler_params=pltpu.CompilerParams(vmem_limit_bytes=8 * 2**20),
        name="update",
    )(arrived, *state)


def code_group(delta, coef_num):
    peers = delta.shape[0]
    me = lax.axis_index("peer")
    held = delta[:, None]
    source = [0]
    step = peers // 2
    while step >= 1:
        high = jnp.bitwise_and(me, step) != 0
        low_half, high_half = held[:step], held[step:]
        keep = jnp.where(high, high_half, low_half)
        send = jnp.where(high, low_half, high_half)
        got = lax.ppermute(send, "peer", [(i, i ^ step) for i in range(peers)])
        held = jnp.concatenate([keep, got], axis=1)
        source = source + [at ^ step for at in source]
        step //= 2
    order = jnp.bitwise_xor(me, jnp.array(source, jnp.int32))
    coef = coef_num.astype(jnp.float32) / 8.0
    picker = (jnp.arange(peers, dtype=jnp.int32)[None, :] == order[:, None]).astype(jnp.float32)
    column = jnp.sum(coef[:, None, :] * picker[None], axis=2)
    return jnp.sum(column[:, :, None, None] * held[0][None], axis=1)


def body(grads, params, moment1, moment2, base_params, base_m1, base_m2, coef_num):
    _, layers, rows, width = grads.shape
    groups = lax.axis_size("dp")
    peers = lax.axis_size("peer")
    own = params.shape
    span = own[2]
    per_row = width // span
    blocks = span // LANES
    tall = (layers * blocks, LANES)

    pieces = grads.reshape(layers, rows, per_row, blocks, LANES)
    pieces = pieces.transpose(1, 2, 0, 3, 4).reshape(groups, *tall)
    arrived = lax.all_to_all(pieces, "dp", 0, 0, tiled=True)

    state = (params, moment1, moment2, base_params, base_m1, base_m2)
    new_params, new_m1, new_m2, spread, delta = update(
        arrived, *(array.reshape(tall) for array in state)
    )

    gathered = lax.all_to_all(spread, "dp", 0, 0, tiled=True)
    weights = gathered.reshape(rows, per_row, layers, blocks, LANES)
    weights = weights.transpose(2, 0, 1, 3, 4).reshape(layers, rows, width)

    parity = code_group(delta, coef_num)
    parity = parity.reshape(parity.shape[0], 3, layers, span // peers)

    return (new_params.reshape(own), new_m1.reshape(own), new_m2.reshape(own), weights, parity)


def solution(mesh):
    state = P(None, "peer", "dp")
    return jax.shard_map(
        body,
        mesh=mesh,
        in_specs=(P("dp", None, "peer", None),) + (state,) * 6 + (P(),),
        out_specs=(
            state,
            state,
            state,
            P(None, "peer", None),
            P(None, None, None, ("dp", "peer")),
        ),
        check_vma=False,
    )
```

time: 93.5 us -> 78.2 us (0.84)
  the two profiles are of different devices: /device:TPU:2 before, /device:TPU:1 now
where the time goes in v2:
time: 78.2 us; the launch traced here: 77.8 us
  starting transfers between devices  50 us (64%)
  waiting for transfers between devices  21.8 us (28%)
  local copies, waits for them, and re-layouts  3.86 us (5%)
  Pallas kernels  1.02 us (1%)
  between operations  0.81 us (1%)
    all_to_all x1, starting transfers between devices, body(): arrived = lax.all_to_all(pieces, 'dp', 0, 0, tiled=True)  25.7 us
    all_to_all x1, waiting for transfers between devices, body(): arrived = lax.all_to_all(pieces, 'dp', 0, 0, tiled=True)  18 us
    ppermute x3, starting transfers between devices, code_group(): got = lax.ppermute(send, 'peer', [(i, i ^ step) for i in range(peers)])  16.4 us
    all_to_all x1, starting transfers between devices, body(): gathered = lax.all_to_all(spread, 'dp', 0, 0, tiled=True)  7.93 us
    ppermute x3, waiting for transfers between devices, code_group(): got = lax.ppermute(send, 'peer', [(i, i ^ step) for i in range(peers)])  3.78 us
    unnamed x18, local copies, waits for them, and re-layouts  1.8 us
  transfers between devices with their start and end apart: 5, of which 4 were waited for; matrix products, arithmetic and copies ran while one was open for 1% of the time, Pallas kernels for 0%

profile of v2, /device:TPU:1, one launch (start us, length us, event | category | flops | bytes accessed | tf_op | source)
XLA Modules:
  0.0 77.8 jit_solution(11424175471870302588)
XLA Ops:
  0.6 1.2 %copy.33 = bf16[4,8,64,128]{3,2,1,0:T(8,128)(2,1)S(1)} copy(bf16[4,8,64,128]{3,1,2,0:T(8,128)(2,1)} %bitcast.37) | data formatting | bytes 1048576
  1.8 0.9 %copy.25 = bf16[2,16,8,8,128]{4,3,0,2,1:T(8,128)(2,1)} copy(bf16[2,16,8,8,128]{4,3,2,1,0:T(8,128)(2,1)S(1)} %bitcast.36) | data formatting | bytes 1048576 | tf_op jit(solution)/shard_map/reshape | solution.py:94
  2.7 0.0 copy-start.7
  2.7 0.0 copy-start.2
  2.7 0.0 copy-start.5
  2.7 25.7 %all-to-all-start = ((bf16[128,16,128]{2,1,0:T(8,128)(2,1)}), bf16[128,16,128]{2,1,0:T(8,128)(2,1)S(1)}, u32[]{:S(2)}, u32[]{:S(2)}) async-start(bf16[128,16,128]{2,1,0:T(8,128)(2,1)} %bitcast.1), calls=%async_computation | async-start | bytes 1048576 | tf_op jit(solution)/shard_map/all_to_all | solution.py:96
  28.4 0.0 copy-start.1
  28.4 0.0 copy-start
  28.4 0.0 copy-done.7
  28.4 18.0 %all-to-all-done.arrived = bf16[128,16,128]{2,1,0:T(8,128)(2,1)S(1)} async-done(((bf16[128,16,128]{2,1,0:T(8,128)(2,1)}), bf16[128,16,128]{2,1,0:T(8,128)(2,1)S(1)}, u32[]{:S(2)}, u32[]{:S(2)}) %all-to-all-start) | async-done | bytes 524320 | tf_op jit(solution)/shard_map/all_to_all | solution.py:96
  46.4 0.0 copy-done.2
  46.4 0.0 copy-done.3
  46.4 0.0 copy-done.4
  46.4 0.0 copy-done.5
  46.4 0.0 copy-done.1
  46.4 0.0 copy-done
  46.5 1.0 %update.1 = (f32[16,128]{1,0:T(8,128)}, f32[16,128]{1,0:T(8,128)}, f32[16,128]{1,0:T(8,128)}, bf16[128,16,128]{2,1,0:T(8,128)(2,1)}, f32[8,6,128]{2,1,0:T(8,128)S(1)}) custom-call(bf16[128,16,128]{2,1,0:T(8,128)(2,1)S(1)} %all-to-all-done.arrived, f32[16,128]{1,0:T(8,128)S(1)} %bitcast.29, f32[16,128]{1,0:T(8,128)S(1)} %bitcast.30, f32[16,128]{1,0:T(8,128)S(1)} %bitcast.31, ...), custom_call_target="tpu_custom_call" | custom-call | tf_op jit(solution)/shard_map/update/pallas_call | solution.py:46
  47.5 7.9 %all-to-all-start.1 = ((bf16[128,16,128]{2,1,0:T(8,128)(2,1)}), bf16[128,16,128]{2,1,0:T(8,128)(2,1)S(1)}, u32[]{:S(2)}, u32[]{:S(2)}) async-start(bf16[128,16,128]{2,1,0:T(8,128)(2,1)} %get-tuple-element.13), calls=%async_computation.1 | async-start | bytes 1048576 | tf_op jit(solution)/shard_map/all_to_all | solution.py:103
  55.4 7.0 %collective-permute-start = (f32[4,1,6,128]{3,2,0,1:T(8,128)S(1)}, f32[4,1,6,128]{3,2,0,1:T(8,128)S(1)}, u32[]{:S(2)}, u32[]{:S(2)}) collective-permute-start(f32[4,1,6,128]{3,2,0,1:T(8,128)S(1)} %get-tuple-element.35), channel_id=1, source_target_pairs={{0,4},{1,5},{2,6},{3,7},{4,0},{5,1},{6,2},{7,3},{8,12},{9,13},{10,... | collective-permute-start | bytes 36872 | tf_op jit(solution)/shard_map/ppermute | solution.py:73
  62.5 0.1 fusion.2
  62.5 1.7 %collective-permute-done = f32[4,1,6,128]{3,2,0,1:T(8,128)S(1)} collective-permute-done((f32[4,1,6,128]{3,2,0,1:T(8,128)S(1)}, f32[4,1,6,128]{3,2,0,1:T(8,128)S(1)}, u32[]{:S(2)}, u32[]{:S(2)}) %collective-permute-start) | collective-permute-done | bytes 12320 | tf_op jit(solution)/shard_map/ppermute | solution.py:73
  64.2 4.4 %collective-permute-start.1 = (f32[2,2,6,128]{3,2,0,1:T(8,128)S(1)}, f32[2,2,6,128]{3,2,0,1:T(8,128)S(1)}, u32[]{:S(2)}, u32[]{:S(2)}) collective-permute-start(f32[2,2,6,128]{3,2,0,1:T(8,128)S(1)} %get-tuple-element.33), channel_id=1, source_target_pairs={{0,2},{1,3},{2,0},{3,1},{4,6},{5,7},{6,4},{7,5},{8,10},{9,11},{10,... | collective-permute-start | bytes 36872 | tf_op jit(solution)/shard_map/ppermute | solution.py:73
  68.7 0.0 copy-done.6
  68.7 1.4 %collective-permute-done.1 = f32[2,2,6,128]{3,2,0,1:T(8,128)S(1)} collective-permute-done((f32[2,2,6,128]{3,2,0,1:T(8,128)S(1)}, f32[2,2,6,128]{3,2,0,1:T(8,128)S(1)}, u32[]{:S(2)}, u32[]{:S(2)}) %collective-permute-start.1) | collective-permute-done | bytes 12320 | tf_op jit(solution)/shard_map/ppermute | solution.py:73
  70.1 5.0 %collective-permute-start.2 = (f32[1,4,6,128]{3,2,0,1:T(8,128)S(1)}, f32[1,4,6,128]{3,2,0,1:T(8,128)S(1)}, u32[]{:S(2)}, u32[]{:S(2)}) collective-permute-start(f32[1,4,6,128]{3,2,0,1:T(8,128)S(1)} %get-tuple-element.31), channel_id=1, source_target_pairs={{0,1},{1,0},{2,3},{3,2},{4,5},{5,4},{6,7},{7,6},{8,9},{9,8},{10,11... | collective-permute-start | bytes 36872 | tf_op jit(solution)/shard_map/ppermute | solution.py:73
  75.1 0.1 multiply_reduce_fusion.1
  75.2 0.7 collective-permute-done.2
  75.9 0.1 multiply_reduce_fusion
  76.0 0.6 copy.32
  76.6 0.0 all-to-all-done.1
  76.6 0.1 copy.26
  76.8 1.0 %reshape.89 = bf16[2,16,8192]{2,1,0:T(8,128)(2,1)} reshape(bf16[2,16,8,8,128]{4,3,2,1,0:T(8,128)(2,1)S(1)} %copy.26) | data formatting | bytes 1048576 | tf_op jit(solution)/shard_map/reshape | solution.py:105
  (11 shorter events, 0.1 us)
Async XLA Ops:
  2.7 25.7 %copy-start.7 = (s32[8]{0:T(128)S(1)}, s32[8]{0:T(128)}, u32[]{:S(2)}) copy-start(s32[8]{0:T(128)} %constant.19.clone) | copy-start | bytes 100
  2.7 43.7 %copy-start.2 = (f32[2,1,1024]{2,1,0:T(1,128)S(1)}, f32[2,1,1024]{2,1,0:T(1,128)}, u32[]{:S(2)}) copy-start(f32[2,1,1024]{2,1,0:T(1,128)} %param.12) | copy-start | bytes 24580
  2.7 43.7 %copy-start.3 = (f32[2,1,1024]{2,1,0:T(1,128)S(1)}, f32[2,1,1024]{2,1,0:T(1,128)}, u32[]{:S(2)}) copy-start(f32[2,1,1024]{2,1,0:T(1,128)} %param.13) | copy-start | bytes 24580
  2.7 43.7 %copy-start.4 = (f32[2,1,1024]{2,1,0:T(1,128)S(1)}, f32[2,1,1024]{2,1,0:T(1,128)}, u32[]{:S(2)}) copy-start(f32[2,1,1024]{2,1,0:T(1,128)} %param.14) | copy-start | bytes 24580
  2.7 43.7 %copy-start.5 = (f32[2,1,1024]{2,1,0:T(1,128)S(1)}, f32[2,1,1024]{2,1,0:T(1,128)}, u32[]{:S(2)}) copy-start(f32[2,1,1024]{2,1,0:T(1,128)} %param.15) | copy-start | bytes 24580
  2.7 43.7 %all-to-all-start = ((bf16[128,16,128]{2,1,0:T(8,128)(2,1)}), bf16[128,16,128]{2,1,0:T(8,128)(2,1)S(1)}, u32[]{:S(2)}, u32[]{:S(2)}) async-start(bf16[128,16,128]{2,1,0:T(8,128)(2,1)} %bitcast.1), calls=%async_computation | async-start | bytes 1048576 | tf_op jit(solution)/shard_map/all_to_all | solution.py:96
  28.4 18.1 %copy-start.1 = (f32[2,1,1024]{2,1,0:T(1,128)S(1)}, f32[2,1,1024]{2,1,0:T(1,128)}, u32[]{:S(2)}) copy-start(f32[2,1,1024]{2,1,0:T(1,128)} %param.11) | copy-start | bytes 24580
  28.4 18.1 %copy-start = (f32[2,1,1024]{2,1,0:T(1,128)S(1)}, f32[2,1,1024]{2,1,0:T(1,128)}, u32[]{:S(2)}) copy-start(f32[2,1,1024]{2,1,0:T(1,128)} %param.10) | copy-start | bytes 24580
  47.5 29.2 %all-to-all-start.1 = ((bf16[128,16,128]{2,1,0:T(8,128)(2,1)}), bf16[128,16,128]{2,1,0:T(8,128)(2,1)S(1)}, u32[]{:S(2)}, u32[]{:S(2)}) async-start(bf16[128,16,128]{2,1,0:T(8,128)(2,1)} %get-tuple-element.13), calls=%async_computation.1 | async-start | bytes 1048576 | tf_op jit(solution)/shard_map/all_to_all | solution.py:103
  55.4 8.8 %collective-permute-start = (f32[4,1,6,128]{3,2,0,1:T(8,128)S(1)}, f32[4,1,6,128]{3,2,0,1:T(8,128)S(1)}, u32[]{:S(2)}, u32[]{:S(2)}) collective-permute-start(f32[4,1,6,128]{3,2,0,1:T(8,128)S(1)} %get-tuple-element.35), channel_id=1, source_target_pairs={{0,4},{1,5},{2,6},{3,7},{4,0},{5,1},{6,2},{7,3},{8,12},{9,13},{10,... | collective-permute-start | bytes 36872 | tf_op jit(solution)/shard_map/ppermute | solution.py:73
  64.2 4.5 %copy-start.6 = (s32[4,8]{1,0:T(4,128)S(1)}, s32[4,8]{1,0:T(4,128)}, u32[]{:S(2)}) copy-start(s32[4,8]{1,0:T(4,128)} %param.16) | copy-start | bytes 388
  64.2 5.9 %collective-permute-start.1 = (f32[2,2,6,128]{3,2,0,1:T(8,128)S(1)}, f32[2,2,6,128]{3,2,0,1:T(8,128)S(1)}, u32[]{:S(2)}, u32[]{:S(2)}) collective-permute-start(f32[2,2,6,128]{3,2,0,1:T(8,128)S(1)} %get-tuple-element.33), channel_id=1, source_target_pairs={{0,2},{1,3},{2,0},{3,1},{4,6},{5,7},{6,4},{7,5},{8,10},{9,11},{10,... | collective-permute-start | bytes 36872 | tf_op jit(solution)/shard_map/ppermute | solution.py:73
  70.1 5.8 %collective-permute-start.2 = (f32[1,4,6,128]{3,2,0,1:T(8,128)S(1)}, f32[1,4,6,128]{3,2,0,1:T(8,128)S(1)}, u32[]{:S(2)}, u32[]{:S(2)}) collective-permute-start(f32[1,4,6,128]{3,2,0,1:T(8,128)S(1)} %get-tuple-element.31), channel_id=1, source_target_pairs={{0,1},{1,0},{2,3},{3,2},{4,5},{5,4},{6,7},{7,6},{8,9},{9,8},{10,11... | collective-permute-start | bytes 36872 | tf_op jit(solution)/shard_map/ppermute | solution.py:73

commit v3 on v2

--- a/solution.py
+++ b/solution.py
@@ -19,6 +19,18 @@
     return (new_params, new_m1, new_m2)
 
 
+def ring(peer):
+    return peer ^ ((peer & 4) >> 1)
+
+
+def halving_order(peers):
+    slots, step = [0], peers // 2
+    while step >= 1:
+        slots = slots + [at + step for at in slots]
+        step //= 2
+    return [slots[ring(j)] for j in range(peers)]
+
+
 def update_kernel(
     arrived, params, moment1, moment2, base_params, base_m1, base_m2,
     new_params, new_m1, new_m2, spread, delta,
@@ -31,11 +43,12 @@
     new_params[...] = p
     new_m1[...] = m1
     new_m2[...] = m2
+    slots = halving_order(peers)
     changes = (p - base_params[...], m1 - base_m1[...], m2 - base_m2[...])
     for s, change in enumerate(changes):
         for l in range(layers):
             for j in range(peers):
-                delta[j, s * layers + l, :] = change[l * peers + j, :]
+                delta[slots[j], s * layers + l, :] = change[l * peers + j, :]
 
 
 def update(arrived, *state):
@@ -61,20 +74,19 @@
 
 def code_group(delta, coef_num):
     peers = delta.shape[0]
-    me = lax.axis_index("peer")
+    delta, me = lax.optimization_barrier((delta, lax.axis_index("peer")))
     held = delta[:, None]
-    source = [0]
-    step = peers // 2
-    while step >= 1:
-        high = jnp.bitwise_and(me, step) != 0
-        low_half, high_half = held[:step], held[step:]
+    label = ring(me)
+    step = 1
+    while step < peers:
+        high = jnp.bitwise_and(label, step) != 0
+        low_half, high_half = jnp.split(held, 2, axis=0)
         keep = jnp.where(high, high_half, low_half)
         send = jnp.where(high, low_half, high_half)
-        got = lax.ppermute(send, "peer", [(i, i ^ step) for i in range(peers)])
+        got = lax.ppermute(send, "peer", [(i, i ^ ring(step)) for i in range(peers)])
         held = jnp.concatenate([keep, got], axis=1)
-        source = source + [at ^ step for at in source]
-        step //= 2
-    order = jnp.bitwise_xor(me, jnp.array(source, jnp.int32))
+        step *= 2
+    order = ring(jnp.bitwise_xor(label, jnp.arange(peers, dtype=jnp.int32)))
     coef = coef_num.astype(jnp.float32) / 8.0
     picker = (jnp.arange(peers, dtype=jnp.int32)[None, :] == order[:, None]).astype(jnp.float32)
     column = jnp.sum(coef[:, None, :] * picker[None], axis=2)
@@ -104,6 +116,7 @@
     weights = gathered.reshape(rows, per_row, layers, blocks, LANES)
     weights = weights.transpose(2, 0, 1, 3, 4).reshape(layers, rows, width)
 
+    delta, coef_num = lax.optimization_barrier((delta, coef_num))
     parity = code_group(delta, coef_num)
     parity = parity.reshape(parity.shape[0], 3, layers, span // peers)
 

time: 78.2 us -> 76.8 us (0.982)
  the two profiles are of different devices: /device:TPU:1 before, /device:TPU:32 now
where the time goes in v3:
time: 76.8 us; the launch traced here: 76.4 us
  starting transfers between devices  40.3 us (52%)
  waiting for transfers between devices  30.1 us (39%)
  local copies, waits for them, and re-layouts  3.85 us (5%)
  Pallas kernels  1.02 us (1%)
  between operations  0.79 us (1%)
    all_to_all x1, starting transfers between devices, body(): arrived = lax.all_to_all(pieces, 'dp', 0, 0, tiled=True)  25.1 us
    all_to_all x1, waiting for transfers between devices, body(): arrived = lax.all_to_all(pieces, 'dp', 0, 0, tiled=True)  20.3 us
    ppermute x3, starting transfers between devices, code_group(): lax.ppermute(send, 'peer', [(i, i ^ ring(step)) for i in range(peers)])  9.06 us
    ppermute x3, waiting for transfers between devices, code_group(): lax.ppermute(send, 'peer', [(i, i ^ ring(step)) for i in range(peers)])  8.12 us
    all_to_all x1, starting transfers between devices, body(): gathered = lax.all_to_all(spread, 'dp', 0, 0, tiled=True)  6.18 us
    unnamed x16, local copies, waits for them, and re-layouts  1.79 us
    all_to_all x1, waiting for transfers between devices, body(): gathered = lax.all_to_all(spread, 'dp', 0, 0, tiled=True)  1.64 us
  transfers between devices with their start and end apart: 5, of which 5 were waited for; matrix products, arithmetic and copies ran while one was open for 1% of the time, Pallas kernels for 0%

profile of v3, /device:TPU:32, one launch (start us, length us, event | category | flops | bytes accessed | tf_op | source)
XLA Modules:
  0.0 76.4 jit_solution(11627088695867219810)
XLA Ops:
  0.6 1.2 %copy.32 = bf16[4,8,64,128]{3,2,1,0:T(8,128)(2,1)S(1)} copy(bf16[4,8,64,128]{3,1,2,0:T(8,128)(2,1)} %bitcast.37) | data formatting | bytes 1048576
  1.8 0.9 %copy.24 = bf16[2,16,8,8,128]{4,3,0,2,1:T(8,128)(2,1)} copy(bf16[2,16,8,8,128]{4,3,2,1,0:T(8,128)(2,1)S(1)} %bitcast.36) | data formatting | bytes 1048576 | tf_op jit(solution)/shard_map/reshape | solution.py:106
  2.7 0.0 copy-start.2
  2.7 0.0 copy-start.3
  2.7 0.0 copy-start.4
  2.7 0.0 copy-start.5
  2.7 25.1 %all-to-all-start = ((bf16[128,16,128]{2,1,0:T(8,128)(2,1)}), bf16[128,16,128]{2,1,0:T(8,128)(2,1)S(1)}, u32[]{:S(2)}, u32[]{:S(2)}) async-start(bf16[128,16,128]{2,1,0:T(8,128)(2,1)} %bitcast.1), calls=%async_computation | async-start | bytes 1048576 | tf_op jit(solution)/shard_map/all_to_all | solution.py:108
  27.8 0.0 copy-start.1
  27.8 0.0 copy-start
  27.8 20.3 %all-to-all-done.arrived = bf16[128,16,128]{2,1,0:T(8,128)(2,1)S(1)} async-done(((bf16[128,16,128]{2,1,0:T(8,128)(2,1)}), bf16[128,16,128]{2,1,0:T(8,128)(2,1)S(1)}, u32[]{:S(2)}, u32[]{:S(2)}) %all-to-all-start) | async-done | bytes 524320 | tf_op jit(solution)/shard_map/all_to_all | solution.py:108
  48.1 0.0 copy-done.2
  48.1 0.0 copy-done.3
  48.2 0.0 copy-done.4
  48.2 0.0 copy-done.5
  48.2 0.0 copy-done.1
  48.2 0.0 copy-done
  48.2 1.0 %update.1 = (f32[16,128]{1,0:T(8,128)}, f32[16,128]{1,0:T(8,128)}, f32[16,128]{1,0:T(8,128)}, bf16[128,16,128]{2,1,0:T(8,128)(2,1)}, f32[8,6,128]{2,1,0:T(8,128)S(1)}) custom-call(bf16[128,16,128]{2,1,0:T(8,128)(2,1)S(1)} %all-to-all-done.arrived, f32[16,128]{1,0:T(8,128)S(1)} %bitcast.29, f32[16,128]{1,0:T(8,128)S(1)} %bitcast.30, f32[16,128]{1,0:T(8,128)S(1)} %bitcast.31, ...), custom_call_target="tpu_custom_call" | custom-call | tf_op jit(solution)/shard_map/update/pallas_call | solution.py:59
  49.2 6.2 %all-to-all-start.1 = ((bf16[128,16,128]{2,1,0:T(8,128)(2,1)}), bf16[128,16,128]{2,1,0:T(8,128)(2,1)S(1)}, u32[]{:S(2)}, u32[]{:S(2)}) async-start(bf16[128,16,128]{2,1,0:T(8,128)(2,1)} %get-tuple-element.17), calls=%async_computation.1 | async-start | bytes 1048576 | tf_op jit(solution)/shard_map/all_to_all | solution.py:115
  55.4 1.9 %collective-permute-start = (f32[4,1,6,128]{3,2,0,1:T(8,128)S(1)}, f32[4,1,6,128]{3,2,0,1:T(8,128)S(1)}, u32[]{:S(2)}, u32[]{:S(2)}) collective-permute-start(f32[4,1,6,128]{3,2,0,1:T(8,128)S(1)} %get-tuple-element.43), channel_id=1, source_target_pairs={{0,1},{1,0},{2,3},{3,2},{4,5},{5,4},{6,7},{7,6},{8,9},{9,8},{10,11... | collective-permute-start | bytes 36872 | tf_op jit(solution)/shard_map/ppermute | solution.py:86
  57.4 0.1 fusion.2
  57.4 1.1 %collective-permute-done = f32[4,1,6,128]{3,2,0,1:T(8,128)S(1)} collective-permute-done((f32[4,1,6,128]{3,2,0,1:T(8,128)S(1)}, f32[4,1,6,128]{3,2,0,1:T(8,128)S(1)}, u32[]{:S(2)}, u32[]{:S(2)}) %collective-permute-start) | collective-permute-done | bytes 12320 | tf_op jit(solution)/shard_map/ppermute | solution.py:86
  58.5 2.0 %collective-permute-start.1 = (f32[2,2,6,128]{3,2,0,1:T(8,128)S(1)}, f32[2,2,6,128]{3,2,0,1:T(8,128)S(1)}, u32[]{:S(2)}, u32[]{:S(2)}) collective-permute-start(f32[2,2,6,128]{3,2,0,1:T(8,128)S(1)} %get-tuple-element.41), channel_id=1, source_target_pairs={{0,2},{1,3},{2,0},{3,1},{4,6},{5,7},{6,4},{7,5},{8,10},{9,11},{10,... | collective-permute-start | bytes 36872 | tf_op jit(solution)/shard_map/ppermute | solution.py:86
  60.5 0.0 copy-done.6
  60.6 4.5 %collective-permute-done.1 = f32[2,2,6,128]{3,2,0,1:T(8,128)S(1)} collective-permute-done((f32[2,2,6,128]{3,2,0,1:T(8,128)S(1)}, f32[2,2,6,128]{3,2,0,1:T(8,128)S(1)}, u32[]{:S(2)}, u32[]{:S(2)}) %collective-permute-start.1) | collective-permute-done | bytes 12320 | tf_op jit(solution)/shard_map/ppermute | solution.py:86
  65.1 5.1 %collective-permute-start.2 = (f32[1,4,6,128]{3,2,0,1:T(8,128)S(1)}, f32[1,4,6,128]{3,2,0,1:T(8,128)S(1)}, u32[]{:S(2)}, u32[]{:S(2)}) collective-permute-start(f32[1,4,6,128]{3,2,0,1:T(8,128)S(1)} %get-tuple-element.39), channel_id=1, source_target_pairs={{0,6},{1,7},{2,4},{3,5},{4,2},{5,3},{6,0},{7,1},{8,14},{9,15},{10,... | collective-permute-start | bytes 36872 | tf_op jit(solution)/shard_map/ppermute | solution.py:86
  70.2 0.1 multiply_reduce_fusion.1
  70.3 2.5 %collective-permute-done.2 = f32[1,4,6,128]{3,2,0,1:T(8,128)S(1)} collective-permute-done((f32[1,4,6,128]{3,2,0,1:T(8,128)S(1)}, f32[1,4,6,128]{3,2,0,1:T(8,128)S(1)}, u32[]{:S(2)}, u32[]{:S(2)}) %collective-permute-start.2) | collective-permute-done | bytes 12320 | tf_op jit(solution)/shard_map/ppermute | solution.py:86
  72.9 0.1 multiply_reduce_fusion
  73.0 0.6 copy.31
  73.6 1.6 %all-to-all-done.1 = bf16[128,16,128]{2,1,0:T(8,128)(2,1)S(1)} async-done(((bf16[128,16,128]{2,1,0:T(8,128)(2,1)}), bf16[128,16,128]{2,1,0:T(8,128)(2,1)S(1)}, u32[]{:S(2)}, u32[]{:S(2)}) %all-to-all-start.1) | async-done | bytes 524320 | tf_op jit(solution)/shard_map/all_to_all | solution.py:115
  75.2 0.1 copy.25
  75.4 1.0 %reshape.97 = bf16[2,16,8192]{2,1,0:T(8,128)(2,1)} reshape(bf16[2,16,8,8,128]{4,3,2,1,0:T(8,128)(2,1)S(1)} %copy.25) | data formatting | bytes 1048576 | tf_op jit(solution)/shard_map/reshape | solution.py:117
  (9 shorter events, 0.1 us)
Async XLA Ops:
  2.7 45.5 %copy-start.2 = (f32[2,1,1024]{2,1,0:T(1,128)S(1)}, f32[2,1,1024]{2,1,0:T(1,128)}, u32[]{:S(2)}) copy-start(f32[2,1,1024]{2,1,0:T(1,128)} %param.11) | copy-start | bytes 24580
  2.7 45.5 %copy-start.3 = (f32[2,1,1024]{2,1,0:T(1,128)S(1)}, f32[2,1,1024]{2,1,0:T(1,128)}, u32[]{:S(2)}) copy-start(f32[2,1,1024]{2,1,0:T(1,128)} %param.12) | copy-start | bytes 24580
  2.7 45.5 %copy-start.4 = (f32[2,1,1024]{2,1,0:T(1,128)S(1)}, f32[2,1,1024]{2,1,0:T(1,128)}, u32[]{:S(2)}) copy-start(f32[2,1,1024]{2,1,0:T(1,128)} %param.13) | copy-start | bytes 24580
  2.7 45.5 %copy-start.5 = (f32[2,1,1024]{2,1,0:T(1,128)S(1)}, f32[2,1,1024]{2,1,0:T(1,128)}, u32[]{:S(2)}) copy-start(f32[2,1,1024]{2,1,0:T(1,128)} %param.14) | copy-start | bytes 24580
  2.7 45.5 %all-to-all-start = ((bf16[128,16,128]{2,1,0:T(8,128)(2,1)}), bf16[128,16,128]{2,1,0:T(8,128)(2,1)S(1)}, u32[]{:S(2)}, u32[]{:S(2)}) async-start(bf16[128,16,128]{2,1,0:T(8,128)(2,1)} %bitcast.1), calls=%async_computation | async-start | bytes 1048576 | tf_op jit(solution)/shard_map/all_to_all | solution.py:108
  27.8 20.4 %copy-start.1 = (f32[2,1,1024]{2,1,0:T(1,128)S(1)}, f32[2,1,1024]{2,1,0:T(1,128)}, u32[]{:S(2)}) copy-start(f32[2,1,1024]{2,1,0:T(1,128)} %param.10) | copy-start | bytes 24580
  27.8 20.4 %copy-start = (f32[2,1,1024]{2,1,0:T(1,128)S(1)}, f32[2,1,1024]{2,1,0:T(1,128)}, u32[]{:S(2)}) copy-start(f32[2,1,1024]{2,1,0:T(1,128)} %param.9) | copy-start | bytes 24580
  49.2 26.0 %all-to-all-start.1 = ((bf16[128,16,128]{2,1,0:T(8,128)(2,1)}), bf16[128,16,128]{2,1,0:T(8,128)(2,1)S(1)}, u32[]{:S(2)}, u32[]{:S(2)}) async-start(bf16[128,16,128]{2,1,0:T(8,128)(2,1)} %get-tuple-element.17), calls=%async_computation.1 | async-start | bytes 1048576 | tf_op jit(solution)/shard_map/all_to_all | solution.py:115
  55.4 3.1 %collective-permute-start = (f32[4,1,6,128]{3,2,0,1:T(8,128)S(1)}, f32[4,1,6,128]{3,2,0,1:T(8,128)S(1)}, u32[]{:S(2)}, u32[]{:S(2)}) collective-permute-start(f32[4,1,6,128]{3,2,0,1:T(8,128)S(1)} %get-tuple-element.43), channel_id=1, source_target_pairs={{0,1},{1,0},{2,3},{3,2},{4,5},{5,4},{6,7},{7,6},{8,9},{9,8},{10,11... | collective-permute-start | bytes 36872 | tf_op jit(solution)/shard_map/ppermute | solution.py:86
  58.5 2.0 %copy-start.6 = (s32[4,8]{1,0:T(4,128)S(1)}, s32[4,8]{1,0:T(4,128)}, u32[]{:S(2)}) copy-start(s32[4,8]{1,0:T(4,128)} %param.15) | copy-start | bytes 388
  58.5 6.6 %collective-permute-start.1 = (f32[2,2,6,128]{3,2,0,1:T(8,128)S(1)}, f32[2,2,6,128]{3,2,0,1:T(8,128)S(1)}, u32[]{:S(2)}, u32[]{:S(2)}) collective-permute-start(f32[2,2,6,128]{3,2,0,1:T(8,128)S(1)} %get-tuple-element.41), channel_id=1, source_target_pairs={{0,2},{1,3},{2,0},{3,1},{4,6},{5,7},{6,4},{7,5},{8,10},{9,11},{10,... | collective-permute-start | bytes 36872 | tf_op jit(solution)/shard_map/ppermute | solution.py:86
  65.1 7.7 %collective-permute-start.2 = (f32[1,4,6,128]{3,2,0,1:T(8,128)S(1)}, f32[1,4,6,128]{3,2,0,1:T(8,128)S(1)}, u32[]{:S(2)}, u32[]{:S(2)}) collective-permute-start(f32[1,4,6,128]{3,2,0,1:T(8,128)S(1)} %get-tuple-element.39), channel_id=1, source_target_pairs={{0,6},{1,7},{2,4},{3,5},{4,2},{5,3},{6,0},{7,1},{8,14},{9,15},{10,... | collective-permute-start | bytes 36872 | tf_op jit(solution)/shard_map/ppermute | solution.py:86

commit v4 on v3

--- a/solution.py
+++ b/solution.py
@@ -31,50 +31,97 @@
     return [slots[ring(j)] for j in range(peers)]
 
 
-def update_kernel(
-    arrived, params, moment1, moment2, base_params, base_m1, base_m2,
-    new_params, new_m1, new_m2, spread, delta,
-):
-    layers = 2
+def place_kernel(gathered, weights, wide, ready, departures):
+    layers, rows, width = weights.shape
+    tall = gathered.shape[1]
+    per_row = gathered.shape[0] // rows
+    span = width // per_row
+    blocks = span // LANES
+    stores = []
+    for c in range(per_row):
+        for r in range(rows):
+            wide[c, r * tall : (r + 1) * tall, :] = gathered[r * per_row + c].astype(jnp.float32)
+        for l in range(layers):
+            for k in range(blocks):
+                tile = wide[c, pl.ds(l * blocks + k, rows, stride=tall), :]
+                ready[c, l, :, k * LANES : (k + 1) * LANES] = tile.astype(jnp.bfloat16)
+        stores.append(
+            pltpu.make_async_copy(
+                ready.at[c], weights.at[:, :, pl.ds(c * span, span)], departures.at[c]
+            )
+        )
+        stores[-1].start()
+    for copy in stores:
+        copy.wait()
+
+
+def place(gathered, layers, rows, width):
+    per_row = gathered.shape[0] // rows
+    tall = gathered.shape[1]
+    return pl.pallas_call(
+        place_kernel,
+        out_shape=jax.ShapeDtypeStruct((layers, rows, width), gathered.dtype),
+        in_specs=[pl.BlockSpec(memory_space=pltpu.VMEM)],
+        out_specs=pl.BlockSpec(memory_space=pltpu.HBM),
+        scratch_shapes=[
+            pltpu.VMEM((per_row, rows * tall, LANES), jnp.float32),
+            pltpu.VMEM((per_row, layers, rows, width // per_row), gathered.dtype),
+            pltpu.SemaphoreType.DMA((per_row,)),
+        ],
+        compiler_params=pltpu.CompilerParams(vmem_limit_bytes=8 * 2**20),
+        name="place",
+    )(gathered)
+
+
+def update_kernel(arrived, *refs):
+    state, (new_params, new_m1, new_m2, spread, delta, held, arrivals) = refs[:6], refs[6:]
+    copies = [
+        pltpu.make_async_copy(ref, held.at[at], arrivals.at[at]) for at, ref in enumerate(state)
+    ]
+    for copy in copies:
+        copy.start()
     peers = delta.shape[0]
+    layers = delta.shape[1] // 3
     g = jnp.sum(arrived[...].astype(jnp.float32), axis=0)
-    p, m1, m2 = adamw(g, params[...], moment1[...], moment2[...])
+    for copy in copies:
+        copy.wait()
+    p, m1, m2 = adamw(g, held[0], held[1], held[2])
     spread[...] = jnp.broadcast_to(p.astype(jnp.bfloat16)[None], spread.shape)
     new_params[...] = p
     new_m1[...] = m1
     new_m2[...] = m2
     slots = halving_order(peers)
-    changes = (p - base_params[...], m1 - base_m1[...], m2 - base_m2[...])
+    changes = (p - held[3], m1 - held[4], m2 - held[5])
     for s, change in enumerate(changes):
         for l in range(layers):
             for j in range(peers):
                 delta[slots[j], s * layers + l, :] = change[l * peers + j, :]
 
 
-def update(arrived, *state):
-    groups = arrived.shape[0]
-    tall = arrived.shape[1:]
+def update(arrived, peers, *state):
+    groups, *tall = arrived.shape
+    layers = tall[0] // peers
     whole = pl.BlockSpec(memory_space=pltpu.VMEM)
-    f32 = jax.ShapeDtypeStruct(tall, jnp.float32)
+    f32 = jax.ShapeDtypeStruct(tuple(tall), jnp.float32)
     return pl.pallas_call(
         update_kernel,
         out_shape=(
             f32,
             f32,
             f32,
-            jax.ShapeDtypeStruct((groups, *tall), jnp.bfloat16),
-            jax.ShapeDtypeStruct((8, 6, LANES), jnp.float32),
+            jax.ShapeDtypeStruct(arrived.shape, jnp.bfloat16),
+            jax.ShapeDtypeStruct((peers, 3 * layers, LANES), jnp.float32),
         ),
-        in_specs=[whole] * 7,
+        in_specs=[whole] + [pl.BlockSpec(memory_space=pltpu.HBM)] * 6,
         out_specs=(whole,) * 5,
+        scratch_shapes=[pltpu.VMEM((6, *tall), jnp.float32), pltpu.SemaphoreType.DMA((6,))],
         compiler_params=pltpu.CompilerParams(vmem_limit_bytes=8 * 2**20),
         name="update",
     )(arrived, *state)
 
 
-def code_group(delta, coef_num):
+def code_group(delta, coef_num, me):
     peers = delta.shape[0]
-    delta, me = lax.optimization_barrier((delta, lax.axis_index("peer")))
     held = delta[:, None]
     label = ring(me)
     step = 1
@@ -103,21 +150,21 @@
     blocks = span // LANES
     tall = (layers * blocks, LANES)
 
+    grads, me = lax.optimization_barrier((grads, lax.axis_index("peer")))
     pieces = grads.reshape(layers, rows, per_row, blocks, LANES)
     pieces = pieces.transpose(1, 2, 0, 3, 4).reshape(groups, *tall)
     arrived = lax.all_to_all(pieces, "dp", 0, 0, tiled=True)
 
     state = (params, moment1, moment2, base_params, base_m1, base_m2)
     new_params, new_m1, new_m2, spread, delta = update(
-        arrived, *(array.reshape(tall) for array in state)
+        arrived, peers, *(array.reshape(tall) for array in state)
     )
 
     gathered = lax.all_to_all(spread, "dp", 0, 0, tiled=True)
-    weights = gathered.reshape(rows, per_row, layers, blocks, LANES)
-    weights = weights.transpose(2, 0, 1, 3, 4).reshape(layers, rows, width)
+    weights = place(gathered, layers, rows, width)
 
-    delta, coef_num = lax.optimization_barrier((delta, coef_num))
-    parity = code_group(delta, coef_num)
+    delta, coef_num, me = lax.optimization_barrier((delta, coef_num, me))
+    parity = code_group(delta, coef_num, me)
     parity = parity.reshape(parity.shape[0], 3, layers, span // peers)
 
     return (new_params.reshape(own), new_m1.reshape(own), new_m2.reshape(own), weights, parity)

time: 76.8 us -> 76.6 us (level)
  blocking collectives: 0 us -> 45.2 us
  starting transfers between devices: 40.3 us -> 15.2 us
  waiting for transfers between devices: 30.1 us -> 9.79 us
  local copies, waits for them, and re-layouts: 3.85 us -> 2.57 us
  Pallas kernels: 1.02 us -> 2.19 us
    all_to_all x0 -> x1, blocking collectives: none -> 45.2 us  [body(): arrived = lax.all_to_all(pieces, 'dp', 0, 0, tiled=True)]
    all_to_all x1 -> x0, starting transfers between devices: 25.1 us -> none  [body(): arrived = lax.all_to_all(pieces, 'dp', 0, 0, tiled=True)]
    all_to_all x1 -> x0, waiting for transfers between devices: 20.3 us -> none  [body(): arrived = lax.all_to_all(pieces, 'dp', 0, 0, tiled=True)]
    pallas_call x0 -> x1, Pallas kernels: none -> 1.09 us  [place(): pl.pallas_call(place_kernel, out_shape=jax.ShapeDtypeStruct((layers, rows...]
    reshape x1 -> x0, local copies, waits for them, and re-layouts: 1.02 us -> none  [body(): weights = weights.transpose(2, 0, 1, 3, 4).reshape(layers, rows, width)]
    reshape x1, local copies, waits for them, and re-layouts: 0.89 us -> 0.09 us  [body(): pieces = grads.reshape(layers, rows, per_row, blocks, LANES)]
  transfers between devices with their start and end apart: 5 -> 4, of which waited for: 5 -> 4; matrix products, arithmetic and copies ran while one was open for 1% -> 1% of each run, Pallas kernels for 0% -> 0%
where the time goes in v4:
time: 76.6 us; the launch traced here: 76.1 us
  blocking collectives  45.2 us (59%)
  starting transfers between devices  15.2 us (20%)
  waiting for transfers between devices  9.79 us (13%)
  local copies, waits for them, and re-layouts  2.57 us (3%)
  Pallas kernels  2.19 us (3%)
  between operations  0.81 us (1%)
    all_to_all x1, blocking collectives, body(): arrived = lax.all_to_all(pieces, 'dp', 0, 0, tiled=True)  45.2 us
    ppermute x3, starting transfers between devices, code_group(): lax.ppermute(send, 'peer', [(i, i ^ ring(step)) for i in range(peers)])  9.04 us
    ppermute x3, waiting for transfers between devices, code_group(): lax.ppermute(send, 'peer', [(i, i ^ ring(step)) for i in range(peers)])  8.15 us
    all_to_all x1, starting transfers between devices, body(): gathered = lax.all_to_all(spread, 'dp', 0, 0, tiled=True)  6.19 us
    unnamed x16, local copies, waits for them, and re-layouts  2.46 us
    all_to_all x1, waiting for transfers between devices, body(): gathered = lax.all_to_all(spread, 'dp', 0, 0, tiled=True)  1.64 us
  transfers between devices with their start and end apart: 4, of which 4 were waited for; matrix products, arithmetic and copies ran while one was open for 1% of the time, Pallas kernels for 0%

profile of v4, /device:TPU:32, one launch (start us, length us, event | category | flops | bytes accessed | tf_op | source)
XLA Modules:
  0.0 76.1 jit_solution(14533440818599337246)
XLA Ops:
  0.6 1.2 %copy.29 = bf16[4,8,64,128]{3,2,1,0:T(8,128)(2,1)S(1)} copy(bf16[4,8,64,128]{3,1,2,0:T(8,128)(2,1)} %bitcast.32) | data formatting | bytes 1048576
  1.8 0.1 copy.22
  1.9 0.0 copy-start.1
  1.9 0.0 copy-start.2
  1.9 0.0 copy-start.3
  1.9 0.0 copy-start.4
  1.9 0.0 copy-start.5
  2.0 45.2 %all_to_all.10.arrived = bf16[128,16,128]{2,1,0:T(8,128)(2,1)S(1)} all-to-all(bf16[128,16,128]{2,1,0:T(8,128)(2,1)S(1)} %bitcast.30), channel_id=1, replica_groups=mesh['dp'=128,'peer'=8] {'dp'}, dimensions={0} | all-to-all | bytes 1048576 | tf_op jit(solution)/shard_map/all_to_all | solution.py:156
  47.2 0.0 copy-start
  47.2 0.0 copy-done.1
  47.2 0.0 copy-done.2
  47.2 0.0 copy-done.3
  47.2 0.0 copy-done.4
  47.2 0.0 copy-done.5
  47.2 0.7 copy-done
  47.9 1.1 %update.1 = (f32[16,128]{1,0:T(8,128)}, f32[16,128]{1,0:T(8,128)}, f32[16,128]{1,0:T(8,128)}, bf16[128,16,128]{2,1,0:T(8,128)(2,1)}, f32[8,6,128]{2,1,0:T(8,128)S(1)}) custom-call(bf16[128,16,128]{2,1,0:T(8,128)(2,1)S(1)} %all_to_all.10.arrived, f32[16,128]{1,0:T(8,128)S(1)} %bitcast.24, f32[16,128]{1,0:T(8,128)S(1)} %bitcast.25, f32[16,128]{1,0:T(8,128)S(1)} %bitcast.26, ...), custom_call_target="tpu_custom_call" | custom-call | tf_op jit(solution)/shard_map/update/pallas_call | solution.py:106
  49.0 6.2 %all-to-all-start.1 = ((bf16[128,16,128]{2,1,0:T(8,128)(2,1)}), bf16[128,16,128]{2,1,0:T(8,128)(2,1)S(1)}, u32[]{:S(2)}, u32[]{:S(2)}) async-start(bf16[128,16,128]{2,1,0:T(8,128)(2,1)} %get-tuple-element.19), calls=%async_computation.1 | async-start | bytes 1048576 | tf_op jit(solution)/shard_map/all_to_all | solution.py:163
  55.2 1.9 %collective-permute-start = (f32[4,1,6,128]{3,2,0,1:T(8,128)S(1)}, f32[4,1,6,128]{3,2,0,1:T(8,128)S(1)}, u32[]{:S(2)}, u32[]{:S(2)}) collective-permute-start(f32[4,1,6,128]{3,2,0,1:T(8,128)S(1)} %get-tuple-element.45), channel_id=1, source_target_pairs={{0,1},{1,0},{2,3},{3,2},{4,5},{5,4},{6,7},{7,6},{8,9},{9,8},{10,11... | collective-permute-start | bytes 36872 | tf_op jit(solution)/shard_map/ppermute | solution.py:133
  57.2 0.1 fusion.2
  57.2 1.1 %collective-permute-done = f32[4,1,6,128]{3,2,0,1:T(8,128)S(1)} collective-permute-done((f32[4,1,6,128]{3,2,0,1:T(8,128)S(1)}, f32[4,1,6,128]{3,2,0,1:T(8,128)S(1)}, u32[]{:S(2)}, u32[]{:S(2)}) %collective-permute-start) | collective-permute-done | bytes 12320 | tf_op jit(solution)/shard_map/ppermute | solution.py:133
  58.3 0.0 copy-start.6
  58.3 2.0 %collective-permute-start.1 = (f32[2,2,6,128]{3,2,0,1:T(8,128)S(1)}, f32[2,2,6,128]{3,2,0,1:T(8,128)S(1)}, u32[]{:S(2)}, u32[]{:S(2)}) collective-permute-start(f32[2,2,6,128]{3,2,0,1:T(8,128)S(1)} %get-tuple-element.43), channel_id=1, source_target_pairs={{0,2},{1,3},{2,0},{3,1},{4,6},{5,7},{6,4},{7,5},{8,10},{9,11},{10,... | collective-permute-start | bytes 36872 | tf_op jit(solution)/shard_map/ppermute | solution.py:133
  60.3 0.0 copy-done.6
  60.4 4.5 %collective-permute-done.1 = f32[2,2,6,128]{3,2,0,1:T(8,128)S(1)} collective-permute-done((f32[2,2,6,128]{3,2,0,1:T(8,128)S(1)}, f32[2,2,6,128]{3,2,0,1:T(8,128)S(1)}, u32[]{:S(2)}, u32[]{:S(2)}) %collective-permute-start.1) | collective-permute-done | bytes 12320 | tf_op jit(solution)/shard_map/ppermute | solution.py:133
  64.9 5.1 %collective-permute-start.2 = (f32[1,4,6,128]{3,2,0,1:T(8,128)S(1)}, f32[1,4,6,128]{3,2,0,1:T(8,128)S(1)}, u32[]{:S(2)}, u32[]{:S(2)}) collective-permute-start(f32[1,4,6,128]{3,2,0,1:T(8,128)S(1)} %get-tuple-element.41), channel_id=1, source_target_pairs={{0,6},{1,7},{2,4},{3,5},{4,2},{5,3},{6,0},{7,1},{8,14},{9,15},{10,... | collective-permute-start | bytes 36872 | tf_op jit(solution)/shard_map/ppermute | solution.py:133
  70.0 0.1 multiply_reduce_fusion.1
  70.1 2.5 %collective-permute-done.2 = f32[1,4,6,128]{3,2,0,1:T(8,128)S(1)} collective-permute-done((f32[1,4,6,128]{3,2,0,1:T(8,128)S(1)}, f32[1,4,6,128]{3,2,0,1:T(8,128)S(1)}, u32[]{:S(2)}, u32[]{:S(2)}) %collective-permute-start.2) | collective-permute-done | bytes 12320 | tf_op jit(solution)/shard_map/ppermute | solution.py:133
  72.7 0.1 multiply_reduce_fusion
  72.8 0.6 copy.28
  73.4 1.6 %all-to-all-done.1.gathered = bf16[128,16,128]{2,1,0:T(8,128)(2,1)S(1)} async-done(((bf16[128,16,128]{2,1,0:T(8,128)(2,1)}), bf16[128,16,128]{2,1,0:T(8,128)(2,1)S(1)}, u32[]{:S(2)}, u32[]{:S(2)}) %all-to-all-start.1) | async-done | bytes 524320 | tf_op jit(solution)/shard_map/all_to_all | solution.py:163
  75.0 1.1 %place.1 = bf16[2,16,8192]{2,1,0:T(8,128)(2,1)} custom-call(bf16[128,16,128]{2,1,0:T(8,128)(2,1)S(1)} %all-to-all-done.1.gathered), custom_call_target="tpu_custom_call" | custom-call | tf_op jit(solution)/shard_map/place/pallas_call | solution.py:61
  (8 shorter events, 0.1 us)
Async XLA Ops:
  1.9 45.3 %copy-start.1 = (f32[2,1,1024]{2,1,0:T(1,128)S(1)}, f32[2,1,1024]{2,1,0:T(1,128)}, u32[]{:S(2)}) copy-start(f32[2,1,1024]{2,1,0:T(1,128)} %param.10) | copy-start | bytes 24580
  1.9 45.3 %copy-start.2 = (f32[2,1,1024]{2,1,0:T(1,128)S(1)}, f32[2,1,1024]{2,1,0:T(1,128)}, u32[]{:S(2)}) copy-start(f32[2,1,1024]{2,1,0:T(1,128)} %param.11) | copy-start | bytes 24580
  1.9 45.3 %copy-start.3 = (f32[2,1,1024]{2,1,0:T(1,128)S(1)}, f32[2,1,1024]{2,1,0:T(1,128)}, u32[]{:S(2)}) copy-start(f32[2,1,1024]{2,1,0:T(1,128)} %param.12) | copy-start | bytes 24580
  1.9 45.3 %copy-start.4 = (f32[2,1,1024]{2,1,0:T(1,128)S(1)}, f32[2,1,1024]{2,1,0:T(1,128)}, u32[]{:S(2)}) copy-start(f32[2,1,1024]{2,1,0:T(1,128)} %param.13) | copy-start | bytes 24580
  1.9 45.3 %copy-start.5 = (f32[2,1,1024]{2,1,0:T(1,128)S(1)}, f32[2,1,1024]{2,1,0:T(1,128)}, u32[]{:S(2)}) copy-start(f32[2,1,1024]{2,1,0:T(1,128)} %param.14) | copy-start | bytes 24580
  47.2 0.7 copy-start
  49.0 26.0 %all-to-all-start.1 = ((bf16[128,16,128]{2,1,0:T(8,128)(2,1)}), bf16[128,16,128]{2,1,0:T(8,128)(2,1)S(1)}, u32[]{:S(2)}, u32[]{:S(2)}) async-start(bf16[128,16,128]{2,1,0:T(8,128)(2,1)} %get-tuple-element.19), calls=%async_computation.1 | async-start | bytes 1048576 | tf_op jit(solution)/shard_map/all_to_all | solution.py:163
  55.2 3.1 %collective-permute-start = (f32[4,1,6,128]{3,2,0,1:T(8,128)S(1)}, f32[4,1,6,128]{3,2,0,1:T(8,128)S(1)}, u32[]{:S(2)}, u32[]{:S(2)}) collective-permute-start(f32[4,1,6,128]{3,2,0,1:T(8,128)S(1)} %get-tuple-element.45), channel_id=1, source_target_pairs={{0,1},{1,0},{2,3},{3,2},{4,5},{5,4},{6,7},{7,6},{8,9},{9,8},{10,11... | collective-permute-start | bytes 36872 | tf_op jit(solution)/shard_map/ppermute | solution.py:133
  58.3 2.0 %copy-start.6 = (s32[4,8]{1,0:T(4,128)S(1)}, s32[4,8]{1,0:T(4,128)}, u32[]{:S(2)}) copy-start(s32[4,8]{1,0:T(4,128)} %param.15) | copy-start | bytes 388
  58.3 6.6 %collective-permute-start.1 = (f32[2,2,6,128]{3,2,0,1:T(8,128)S(1)}, f32[2,2,6,128]{3,2,0,1:T(8,128)S(1)}, u32[]{:S(2)}, u32[]{:S(2)}) collective-permute-start(f32[2,2,6,128]{3,2,0,1:T(8,128)S(1)} %get-tuple-element.43), channel_id=1, source_target_pairs={{0,2},{1,3},{2,0},{3,1},{4,6},{5,7},{6,4},{7,5},{8,10},{9,11},{10,... | collective-permute-start | bytes 36872 | tf_op jit(solution)/shard_map/ppermute | solution.py:133
  64.9 7.7 %collective-permute-start.2 = (f32[1,4,6,128]{3,2,0,1:T(8,128)S(1)}, f32[1,4,6,128]{3,2,0,1:T(8,128)S(1)}, u32[]{:S(2)}, u32[]{:S(2)}) collective-permute-start(f32[1,4,6,128]{3,2,0,1:T(8,128)S(1)} %get-tuple-element.41), channel_id=1, source_target_pairs={{0,6},{1,7},{2,4},{3,5},{4,2},{5,3},{6,0},{7,1},{8,14},{9,15},{10,... | collective-permute-start | bytes 36872 | tf_op jit(solution)/shard_map/ppermute | solution.py:133

commit v5 on v4

--- a/solution.py
+++ b/solution.py
@@ -6,6 +6,11 @@
 from jax.sharding import PartitionSpec as P
 
 LANES = 128
+FIRST = 112
+
+
+def listed(groups):
+    return [[(FIRST + i) % groups for i in range(groups)]]
 
 
 def adamw(g, params, moment1, moment2):
@@ -40,7 +45,9 @@
     stores = []
     for c in range(per_row):
         for r in range(rows):
-            wide[c, r * tall : (r + 1) * tall, :] = gathered[r * per_row + c].astype(jnp.float32)
+            wide[c, r * tall : (r + 1) * tall, :] = gathered[
+                (r - FIRST // per_row) % rows * per_row + c
+            ].astype(jnp.float32)
         for l in range(layers):
             for k in range(blocks):
                 tile = wide[c, pl.ds(l * blocks + k, rows, stride=tall), :]
@@ -152,15 +159,18 @@
 
     grads, me = lax.optimization_barrier((grads, lax.axis_index("peer")))
     pieces = grads.reshape(layers, rows, per_row, blocks, LANES)
-    pieces = pieces.transpose(1, 2, 0, 3, 4).reshape(groups, *tall)
-    arrived = lax.all_to_all(pieces, "dp", 0, 0, tiled=True)
+    pieces = jnp.roll(pieces.transpose(1, 2, 0, 3, 4), -(FIRST // per_row), axis=0)
+    pieces = pieces.reshape(groups, *tall)
+    arrived = lax.all_to_all(pieces, "dp", 0, 0, tiled=True, axis_index_groups=listed(groups))
 
     state = (params, moment1, moment2, base_params, base_m1, base_m2)
     new_params, new_m1, new_m2, spread, delta = update(
         arrived, peers, *(array.reshape(tall) for array in state)
     )
 
-    gathered = lax.all_to_all(spread, "dp", 0, 0, tiled=True)
+    gathered = lax.all_to_all(
+        spread, "dp", 0, 0, tiled=True, axis_index_groups=listed(groups)
+    )
     weights = place(gathered, layers, rows, width)
 
     delta, coef_num, me = lax.optimization_barrier((delta, coef_num, me))

time: 76.6 us -> 74.9 us (0.978)
  the two profiles are of different devices: /device:TPU:32 before, /device:TPU:4 now
where the time goes in v5:
time: 74.9 us; the launch traced here: 74.5 us
  blocking collectives  42.5 us (57%)
  starting transfers between devices  21.3 us (28%)
  waiting for transfers between devices  4.68 us (6%)
  local copies, waits for them, and re-layouts  2.61 us (3%)
  Pallas kernels  2.19 us (3%)
  between operations  0.83 us (1%)
    all_to_all x1, blocking collectives, body(): lax.all_to_all(pieces, 'dp', 0, 0, tiled=True, axis_index_groups=listed(g...  42.5 us
    ppermute x3, starting transfers between devices, code_group(): lax.ppermute(send, 'peer', [(i, i ^ ring(step)) for i in range(peers)])  12.8 us
    all_to_all x1, starting transfers between devices, body(): lax.all_to_all(spread, 'dp', 0, 0, tiled=True, axis_index_groups=listed(g...  8.51 us
    ppermute x3, waiting for transfers between devices, code_group(): lax.ppermute(send, 'peer', [(i, i ^ ring(step)) for i in range(peers)])  4.68 us
    unnamed x16, local copies, waits for them, and re-layouts  2.46 us
  transfers between devices with their start and end apart: 4, of which 3 were waited for; matrix products, arithmetic and copies ran while one was open for 1% of the time, Pallas kernels for 0%

profile of v5, /device:TPU:4, one launch (start us, length us, event | category | flops | bytes accessed | tf_op | source)
XLA Modules:
  0.0 74.5 jit_solution(5298056654811644226)
XLA Ops:
  0.6 1.2 %copy.29 = bf16[4,8,64,128]{3,2,1,0:T(8,128)(2,1)S(1)} copy(bf16[4,8,64,128]{3,1,2,0:T(8,128)(2,1)} %bitcast.35) | data formatting | bytes 1048576
  1.8 0.1 copy.31
  2.0 0.0 copy-start.1
  2.0 0.0 copy-start.2
  2.0 0.0 copy-start.3
  2.0 0.0 copy-start.4
  2.1 0.0 copy-start.5
  2.1 42.5 %all_to_all.10.arrived = bf16[128,16,128]{2,1,0:T(8,128)(2,1)S(1)} all-to-all(bf16[128,16,128]{2,1,0:T(8,128)(2,1)S(1)} %bitcast.33), channel_id=1, replica_groups={{896,904,912,920,928,936,944,952,960,968,976,984,992,1000,1008,1016,0,8..., dimensions={0} | all-to-all | bytes 1048576 | tf_op jit(solution)/shard_map/all_to_all | solution.py:164
  44.6 0.0 copy-start
  44.6 0.0 copy-done.1
  44.6 0.0 copy-done.2
  44.6 0.0 copy-done.3
  44.6 0.0 copy-done.4
  44.6 0.0 copy-done.5
  44.6 0.7 copy-done
  45.3 1.1 %update.1 = (f32[16,128]{1,0:T(8,128)}, f32[16,128]{1,0:T(8,128)}, f32[16,128]{1,0:T(8,128)}, bf16[128,16,128]{2,1,0:T(8,128)(2,1)}, f32[8,6,128]{2,1,0:T(8,128)S(1)}) custom-call(bf16[128,16,128]{2,1,0:T(8,128)(2,1)S(1)} %all_to_all.10.arrived, f32[16,128]{1,0:T(8,128)S(1)} %bitcast.25, f32[16,128]{1,0:T(8,128)S(1)} %bitcast.26, f32[16,128]{1,0:T(8,128)S(1)} %bitcast.27, ...), custom_call_target="tpu_custom_call" | custom-call | tf_op jit(solution)/shard_map/update/pallas_call | solution.py:113
  46.4 8.5 %all-to-all-start.1 = ((bf16[128,16,128]{2,1,0:T(8,128)(2,1)}), bf16[128,16,128]{2,1,0:T(8,128)(2,1)S(1)}, u32[]{:S(2)}, u32[]{:S(2)}) async-start(bf16[128,16,128]{2,1,0:T(8,128)(2,1)} %get-tuple-element.19), calls=%async_computation.1 | async-start | bytes 1048576 | tf_op jit(solution)/shard_map/all_to_all | solution.py:171
  55.0 1.9 %collective-permute-start = (f32[4,1,6,128]{3,2,0,1:T(8,128)S(1)}, f32[4,1,6,128]{3,2,0,1:T(8,128)S(1)}, u32[]{:S(2)}, u32[]{:S(2)}) collective-permute-start(f32[4,1,6,128]{3,2,0,1:T(8,128)S(1)} %get-tuple-element.45), channel_id=1, source_target_pairs={{0,1},{1,0},{2,3},{3,2},{4,5},{5,4},{6,7},{7,6},{8,9},{9,8},{10,11... | collective-permute-start | bytes 36872 | tf_op jit(solution)/shard_map/ppermute | solution.py:140
  56.9 0.1 fusion.2
  57.0 0.0 copy-start.6
  57.0 1.1 %collective-permute-done = f32[4,1,6,128]{3,2,0,1:T(8,128)S(1)} collective-permute-done((f32[4,1,6,128]{3,2,0,1:T(8,128)S(1)}, f32[4,1,6,128]{3,2,0,1:T(8,128)S(1)}, u32[]{:S(2)}, u32[]{:S(2)}) %collective-permute-start) | collective-permute-done | bytes 12320 | tf_op jit(solution)/shard_map/ppermute | solution.py:140
  58.0 4.7 %collective-permute-start.1 = (f32[2,2,6,128]{3,2,0,1:T(8,128)S(1)}, f32[2,2,6,128]{3,2,0,1:T(8,128)S(1)}, u32[]{:S(2)}, u32[]{:S(2)}) collective-permute-start(f32[2,2,6,128]{3,2,0,1:T(8,128)S(1)} %get-tuple-element.43), channel_id=1, source_target_pairs={{0,2},{1,3},{2,0},{3,1},{4,6},{5,7},{6,4},{7,5},{8,10},{9,11},{10,... | collective-permute-start | bytes 36872 | tf_op jit(solution)/shard_map/ppermute | solution.py:140
  62.8 0.0 copy-done.6
  62.8 1.9 %collective-permute-done.1 = f32[2,2,6,128]{3,2,0,1:T(8,128)S(1)} collective-permute-done((f32[2,2,6,128]{3,2,0,1:T(8,128)S(1)}, f32[2,2,6,128]{3,2,0,1:T(8,128)S(1)}, u32[]{:S(2)}, u32[]{:S(2)}) %collective-permute-start.1) | collective-permute-done | bytes 12320 | tf_op jit(solution)/shard_map/ppermute | solution.py:140
  64.7 6.1 %collective-permute-start.2 = (f32[1,4,6,128]{3,2,0,1:T(8,128)S(1)}, f32[1,4,6,128]{3,2,0,1:T(8,128)S(1)}, u32[]{:S(2)}, u32[]{:S(2)}) collective-permute-start(f32[1,4,6,128]{3,2,0,1:T(8,128)S(1)} %get-tuple-element.41), channel_id=1, source_target_pairs={{0,6},{1,7},{2,4},{3,5},{4,2},{5,3},{6,0},{7,1},{8,14},{9,15},{10,... | collective-permute-start | bytes 36872 | tf_op jit(solution)/shard_map/ppermute | solution.py:140
  70.8 0.1 multiply_reduce_fusion.1
  70.9 1.7 %collective-permute-done.2 = f32[1,4,6,128]{3,2,0,1:T(8,128)S(1)} collective-permute-done((f32[1,4,6,128]{3,2,0,1:T(8,128)S(1)}, f32[1,4,6,128]{3,2,0,1:T(8,128)S(1)}, u32[]{:S(2)}, u32[]{:S(2)}) %collective-permute-start.2) | collective-permute-done | bytes 12320 | tf_op jit(solution)/shard_map/ppermute | solution.py:140
  72.6 0.1 multiply_reduce_fusion
  72.8 0.6 copy.28
  73.4 0.0 all-to-all-done.1.gathered
  73.4 1.1 %place.1 = bf16[2,16,8192]{2,1,0:T(8,128)(2,1)} custom-call(bf16[128,16,128]{2,1,0:T(8,128)(2,1)S(1)} %all-to-all-done.1.gathered), custom_call_target="tpu_custom_call" | custom-call | tf_op jit(solution)/shard_map/place/pallas_call | solution.py:68
  (11 shorter events, 0.1 us)
Async XLA Ops:
  2.0 42.6 %copy-start.1 = (f32[2,1,1024]{2,1,0:T(1,128)S(1)}, f32[2,1,1024]{2,1,0:T(1,128)}, u32[]{:S(2)}) copy-start(f32[2,1,1024]{2,1,0:T(1,128)} %param.10) | copy-start | bytes 24580
  2.0 42.6 %copy-start.2 = (f32[2,1,1024]{2,1,0:T(1,128)S(1)}, f32[2,1,1024]{2,1,0:T(1,128)}, u32[]{:S(2)}) copy-start(f32[2,1,1024]{2,1,0:T(1,128)} %param.11) | copy-start | bytes 24580
  2.0 42.6 %copy-start.3 = (f32[2,1,1024]{2,1,0:T(1,128)S(1)}, f32[2,1,1024]{2,1,0:T(1,128)}, u32[]{:S(2)}) copy-start(f32[2,1,1024]{2,1,0:T(1,128)} %param.12) | copy-start | bytes 24580
  2.0 42.6 %copy-start.4 = (f32[2,1,1024]{2,1,0:T(1,128)S(1)}, f32[2,1,1024]{2,1,0:T(1,128)}, u32[]{:S(2)}) copy-start(f32[2,1,1024]{2,1,0:T(1,128)} %param.13) | copy-start | bytes 24580
  2.1 42.6 %copy-start.5 = (f32[2,1,1024]{2,1,0:T(1,128)S(1)}, f32[2,1,1024]{2,1,0:T(1,128)}, u32[]{:S(2)}) copy-start(f32[2,1,1024]{2,1,0:T(1,128)} %param.14) | copy-start | bytes 24580
  44.6 0.7 copy-start
  46.4 27.0 %all-to-all-start.1 = ((bf16[128,16,128]{2,1,0:T(8,128)(2,1)}), bf16[128,16,128]{2,1,0:T(8,128)(2,1)S(1)}, u32[]{:S(2)}, u32[]{:S(2)}) async-start(bf16[128,16,128]{2,1,0:T(8,128)(2,1)} %get-tuple-element.19), calls=%async_computation.1 | async-start | bytes 1048576 | tf_op jit(solution)/shard_map/all_to_all | solution.py:171
  55.0 3.1 %collective-permute-start = (f32[4,1,6,128]{3,2,0,1:T(8,128)S(1)}, f32[4,1,6,128]{3,2,0,1:T(8,128)S(1)}, u32[]{:S(2)}, u32[]{:S(2)}) collective-permute-start(f32[4,1,6,128]{3,2,0,1:T(8,128)S(1)} %get-tuple-element.45), channel_id=1, source_target_pairs={{0,1},{1,0},{2,3},{3,2},{4,5},{5,4},{6,7},{7,6},{8,9},{9,8},{10,11... | collective-permute-start | bytes 36872 | tf_op jit(solution)/shard_map/ppermute | solution.py:140
  57.0 5.8 %copy-start.6 = (s32[4,8]{1,0:T(4,128)S(1)}, s32[4,8]{1,0:T(4,128)}, u32[]{:S(2)}) copy-start(s32[4,8]{1,0:T(4,128)} %param.15) | copy-start | bytes 388
  58.0 6.6 %collective-permute-start.1 = (f32[2,2,6,128]{3,2,0,1:T(8,128)S(1)}, f32[2,2,6,128]{3,2,0,1:T(8,128)S(1)}, u32[]{:S(2)}, u32[]{:S(2)}) collective-permute-start(f32[2,2,6,128]{3,2,0,1:T(8,128)S(1)} %get-tuple-element.43), channel_id=1, source_target_pairs={{0,2},{1,3},{2,0},{3,1},{4,6},{5,7},{6,4},{7,5},{8,10},{9,11},{10,... | collective-permute-start | bytes 36872 | tf_op jit(solution)/shard_map/ppermute | solution.py:140
  64.7 7.9 %collective-permute-start.2 = (f32[1,4,6,128]{3,2,0,1:T(8,128)S(1)}, f32[1,4,6,128]{3,2,0,1:T(8,128)S(1)}, u32[]{:S(2)}, u32[]{:S(2)}) collective-permute-start(f32[1,4,6,128]{3,2,0,1:T(8,128)S(1)} %get-tuple-element.41), channel_id=1, source_target_pairs={{0,6},{1,7},{2,4},{3,5},{4,2},{5,3},{6,0},{7,1},{8,14},{9,15},{10,... | collective-permute-start | bytes 36872 | tf_op jit(solution)/shard_map/ppermute | solution.py:140

commit v6 on v5

--- a/solution.py
+++ b/solution.py
@@ -45,9 +45,7 @@
     stores = []
     for c in range(per_row):
         for r in range(rows):
-            wide[c, r * tall : (r + 1) * tall, :] = gathered[
-                (r - FIRST // per_row) % rows * per_row + c
-            ].astype(jnp.float32)
+            wide[c, r * tall : (r + 1) * tall, :] = gathered[r * per_row + c].astype(jnp.float32)
         for l in range(layers):
             for k in range(blocks):
                 tile = wide[c, pl.ds(l * blocks + k, rows, stride=tall), :]
@@ -168,9 +166,7 @@
         arrived, peers, *(array.reshape(tall) for array in state)
     )
 
-    gathered = lax.all_to_all(
-        spread, "dp", 0, 0, tiled=True, axis_index_groups=listed(groups)
-    )
+    gathered = lax.all_to_all(spread, "dp", 0, 0, tiled=True)
     weights = place(gathered, layers, rows, width)
 
     delta, coef_num, me = lax.optimization_barrier((delta, coef_num, me))

time: 74.9 us -> 76.1 us (1.016)
  the two profiles are of different devices: /device:TPU:4 before, /device:TPU:32 now
where the time goes in v6:
time: 76.1 us; the launch traced here: 75.7 us
  blocking collectives  43.2 us (57%)
  starting transfers between devices  16.5 us (22%)
  waiting for transfers between devices  9.98 us (13%)
  local copies, waits for them, and re-layouts  2.61 us (3%)
  Pallas kernels  2.19 us (3%)
  between operations  0.83 us (1%)
    all_to_all x1, blocking collectives, body(): lax.all_to_all(pieces, 'dp', 0, 0, tiled=True, axis_index_groups=listed(g...  43.2 us
    ppermute x3, starting transfers between devices, code_group(): lax.ppermute(send, 'peer', [(i, i ^ ring(step)) for i in range(peers)])  8.87 us
    ppermute x3, waiting for transfers between devices, code_group(): lax.ppermute(send, 'peer', [(i, i ^ ring(step)) for i in range(peers)])  8.48 us
    all_to_all x1, starting transfers between devices, body(): gathered = lax.all_to_all(spread, 'dp', 0, 0, tiled=True)  7.59 us
    unnamed x16, local copies, waits for them, and re-layouts  2.46 us
  transfers between devices with their start and end apart: 4, of which 4 were waited for; matrix products, arithmetic and copies ran while one was open for 1% of the time, Pallas kernels for 0%

profile of v6, /device:TPU:32, one launch (start us, length us, event | category | flops | bytes accessed | tf_op | source)
XLA Modules:
  0.0 75.7 jit_solution(13605339691550278231)
XLA Ops:
  0.6 1.2 %copy.29 = bf16[4,8,64,128]{3,2,1,0:T(8,128)(2,1)S(1)} copy(bf16[4,8,64,128]{3,1,2,0:T(8,128)(2,1)} %bitcast.35) | data formatting | bytes 1048576
  1.8 0.1 copy.31
  2.0 0.0 copy-start.1
  2.0 0.0 copy-start.2
  2.0 0.0 copy-start.3
  2.0 0.0 copy-start.4
  2.1 0.0 copy-start.5
  2.1 43.2 %all_to_all.10.arrived = bf16[128,16,128]{2,1,0:T(8,128)(2,1)S(1)} all-to-all(bf16[128,16,128]{2,1,0:T(8,128)(2,1)S(1)} %bitcast.33), channel_id=1, replica_groups={{896,904,912,920,928,936,944,952,960,968,976,984,992,1000,1008,1016,0,8..., dimensions={0} | all-to-all | bytes 1048576 | tf_op jit(solution)/shard_map/all_to_all | solution.py:162
  45.3 0.0 copy-start
  45.3 0.0 copy-done.1
  45.3 0.0 copy-done.2
  45.3 0.0 copy-done.3
  45.3 0.0 copy-done.4
  45.3 0.0 copy-done.5
  45.3 0.7 copy-done
  46.0 1.1 %update.1 = (f32[16,128]{1,0:T(8,128)}, f32[16,128]{1,0:T(8,128)}, f32[16,128]{1,0:T(8,128)}, bf16[128,16,128]{2,1,0:T(8,128)(2,1)}, f32[8,6,128]{2,1,0:T(8,128)S(1)}) custom-call(bf16[128,16,128]{2,1,0:T(8,128)(2,1)S(1)} %all_to_all.10.arrived, f32[16,128]{1,0:T(8,128)S(1)} %bitcast.25, f32[16,128]{1,0:T(8,128)S(1)} %bitcast.26, f32[16,128]{1,0:T(8,128)S(1)} %bitcast.27, ...), custom_call_target="tpu_custom_call" | custom-call | tf_op jit(solution)/shard_map/update/pallas_call | solution.py:111
  47.1 7.6 %all-to-all-start.1 = ((bf16[128,16,128]{2,1,0:T(8,128)(2,1)}), bf16[128,16,128]{2,1,0:T(8,128)(2,1)S(1)}, u32[]{:S(2)}, u32[]{:S(2)}) async-start(bf16[128,16,128]{2,1,0:T(8,128)(2,1)} %get-tuple-element.19), calls=%async_computation.1 | async-start | bytes 1048576 | tf_op jit(solution)/shard_map/all_to_all | solution.py:169
  54.7 1.9 %collective-permute-start = (f32[4,1,6,128]{3,2,0,1:T(8,128)S(1)}, f32[4,1,6,128]{3,2,0,1:T(8,128)S(1)}, u32[]{:S(2)}, u32[]{:S(2)}) collective-permute-start(f32[4,1,6,128]{3,2,0,1:T(8,128)S(1)} %get-tuple-element.45), channel_id=1, source_target_pairs={{0,1},{1,0},{2,3},{3,2},{4,5},{5,4},{6,7},{7,6},{8,9},{9,8},{10,11... | collective-permute-start | bytes 36872 | tf_op jit(solution)/shard_map/ppermute | solution.py:138
  56.7 0.1 fusion.2
  56.7 0.0 copy-start.6
  56.7 1.1 %collective-permute-done = f32[4,1,6,128]{3,2,0,1:T(8,128)S(1)} collective-permute-done((f32[4,1,6,128]{3,2,0,1:T(8,128)S(1)}, f32[4,1,6,128]{3,2,0,1:T(8,128)S(1)}, u32[]{:S(2)}, u32[]{:S(2)}) %collective-permute-start) | collective-permute-done | bytes 12320 | tf_op jit(solution)/shard_map/ppermute | solution.py:138
  57.8 2.0 %collective-permute-start.1 = (f32[2,2,6,128]{3,2,0,1:T(8,128)S(1)}, f32[2,2,6,128]{3,2,0,1:T(8,128)S(1)}, u32[]{:S(2)}, u32[]{:S(2)}) collective-permute-start(f32[2,2,6,128]{3,2,0,1:T(8,128)S(1)} %get-tuple-element.43), channel_id=1, source_target_pairs={{0,2},{1,3},{2,0},{3,1},{4,6},{5,7},{6,4},{7,5},{8,10},{9,11},{10,... | collective-permute-start | bytes 36872 | tf_op jit(solution)/shard_map/ppermute | solution.py:138
  59.8 0.0 copy-done.6
  59.9 4.7 %collective-permute-done.1 = f32[2,2,6,128]{3,2,0,1:T(8,128)S(1)} collective-permute-done((f32[2,2,6,128]{3,2,0,1:T(8,128)S(1)}, f32[2,2,6,128]{3,2,0,1:T(8,128)S(1)}, u32[]{:S(2)}, u32[]{:S(2)}) %collective-permute-start.1) | collective-permute-done | bytes 12320 | tf_op jit(solution)/shard_map/ppermute | solution.py:138
  64.6 4.9 %collective-permute-start.2 = (f32[1,4,6,128]{3,2,0,1:T(8,128)S(1)}, f32[1,4,6,128]{3,2,0,1:T(8,128)S(1)}, u32[]{:S(2)}, u32[]{:S(2)}) collective-permute-start(f32[1,4,6,128]{3,2,0,1:T(8,128)S(1)} %get-tuple-element.41), channel_id=1, source_target_pairs={{0,6},{1,7},{2,4},{3,5},{4,2},{5,3},{6,0},{7,1},{8,14},{9,15},{10,... | collective-permute-start | bytes 36872 | tf_op jit(solution)/shard_map/ppermute | solution.py:138
  69.5 0.1 multiply_reduce_fusion.1
  69.6 2.7 %collective-permute-done.2 = f32[1,4,6,128]{3,2,0,1:T(8,128)S(1)} collective-permute-done((f32[1,4,6,128]{3,2,0,1:T(8,128)S(1)}, f32[1,4,6,128]{3,2,0,1:T(8,128)S(1)}, u32[]{:S(2)}, u32[]{:S(2)}) %collective-permute-start.2) | collective-permute-done | bytes 12320 | tf_op jit(solution)/shard_map/ppermute | solution.py:138
  72.3 0.1 multiply_reduce_fusion
  72.5 0.6 copy.28
  73.1 1.5 %all-to-all-done.1.gathered = bf16[128,16,128]{2,1,0:T(8,128)(2,1)S(1)} async-done(((bf16[128,16,128]{2,1,0:T(8,128)(2,1)}), bf16[128,16,128]{2,1,0:T(8,128)(2,1)S(1)}, u32[]{:S(2)}, u32[]{:S(2)}) %all-to-all-start.1) | async-done | bytes 524320 | tf_op jit(solution)/shard_map/all_to_all | solution.py:169
  74.6 1.1 %place.1 = bf16[2,16,8192]{2,1,0:T(8,128)(2,1)} custom-call(bf16[128,16,128]{2,1,0:T(8,128)(2,1)S(1)} %all-to-all-done.1.gathered), custom_call_target="tpu_custom_call" | custom-call | tf_op jit(solution)/shard_map/place/pallas_call | solution.py:66
  (11 shorter events, 0.1 us)
Async XLA Ops:
  2.0 43.3 %copy-start.1 = (f32[2,1,1024]{2,1,0:T(1,128)S(1)}, f32[2,1,1024]{2,1,0:T(1,128)}, u32[]{:S(2)}) copy-start(f32[2,1,1024]{2,1,0:T(1,128)} %param.10) | copy-start | bytes 24580
  2.0 43.3 %copy-start.2 = (f32[2,1,1024]{2,1,0:T(1,128)S(1)}, f32[2,1,1024]{2,1,0:T(1,128)}, u32[]{:S(2)}) copy-start(f32[2,1,1024]{2,1,0:T(1,128)} %param.11) | copy-start | bytes 24580
  2.0 43.3 %copy-start.3 = (f32[2,1,1024]{2,1,0:T(1,128)S(1)}, f32[2,1,1024]{2,1,0:T(1,128)}, u32[]{:S(2)}) copy-start(f32[2,1,1024]{2,1,0:T(1,128)} %param.12) | copy-start | bytes 24580
  2.0 43.3 %copy-start.4 = (f32[2,1,1024]{2,1,0:T(1,128)S(1)}, f32[2,1,1024]{2,1,0:T(1,128)}, u32[]{:S(2)}) copy-start(f32[2,1,1024]{2,1,0:T(1,128)} %param.13) | copy-start | bytes 24580
  2.1 43.3 %copy-start.5 = (f32[2,1,1024]{2,1,0:T(1,128)S(1)}, f32[2,1,1024]{2,1,0:T(1,128)}, u32[]{:S(2)}) copy-start(f32[2,1,1024]{2,1,0:T(1,128)} %param.14) | copy-start | bytes 24580
  45.3 0.7 copy-start
  47.1 27.4 %all-to-all-start.1 = ((bf16[128,16,128]{2,1,0:T(8,128)(2,1)}), bf16[128,16,128]{2,1,0:T(8,128)(2,1)S(1)}, u32[]{:S(2)}, u32[]{:S(2)}) async-start(bf16[128,16,128]{2,1,0:T(8,128)(2,1)} %get-tuple-element.19), calls=%async_computation.1 | async-start | bytes 1048576 | tf_op jit(solution)/shard_map/all_to_all | solution.py:169
  54.7 3.1 %collective-permute-start = (f32[4,1,6,128]{3,2,0,1:T(8,128)S(1)}, f32[4,1,6,128]{3,2,0,1:T(8,128)S(1)}, u32[]{:S(2)}, u32[]{:S(2)}) collective-permute-start(f32[4,1,6,128]{3,2,0,1:T(8,128)S(1)} %get-tuple-element.45), channel_id=1, source_target_pairs={{0,1},{1,0},{2,3},{3,2},{4,5},{5,4},{6,7},{7,6},{8,9},{9,8},{10,11... | collective-permute-start | bytes 36872 | tf_op jit(solution)/shard_map/ppermute | solution.py:138
  56.7 3.1 %copy-start.6 = (s32[4,8]{1,0:T(4,128)S(1)}, s32[4,8]{1,0:T(4,128)}, u32[]{:S(2)}) copy-start(s32[4,8]{1,0:T(4,128)} %param.15) | copy-start | bytes 388
  57.8 6.8 %collective-permute-start.1 = (f32[2,2,6,128]{3,2,0,1:T(8,128)S(1)}, f32[2,2,6,128]{3,2,0,1:T(8,128)S(1)}, u32[]{:S(2)}, u32[]{:S(2)}) collective-permute-start(f32[2,2,6,128]{3,2,0,1:T(8,128)S(1)} %get-tuple-element.43), channel_id=1, source_target_pairs={{0,2},{1,3},{2,0},{3,1},{4,6},{5,7},{6,4},{7,5},{8,10},{9,11},{10,... | collective-permute-start | bytes 36872 | tf_op jit(solution)/shard_map/ppermute | solution.py:138
  64.6 7.7 %collective-permute-start.2 = (f32[1,4,6,128]{3,2,0,1:T(8,128)S(1)}, f32[1,4,6,128]{3,2,0,1:T(8,128)S(1)}, u32[]{:S(2)}, u32[]{:S(2)}) collective-permute-start(f32[1,4,6,128]{3,2,0,1:T(8,128)S(1)} %get-tuple-element.41), channel_id=1, source_target_pairs={{0,6},{1,7},{2,4},{3,5},{4,2},{5,3},{6,0},{7,1},{8,14},{9,15},{10,... | collective-permute-start | bytes 36872 | tf_op jit(solution)/shard_map/ppermute | solution.py:138
